TPU v7x, 32 devices: a whole 2x2x4 slice. The times are simulated.
32 devices in a mesh: grp: 4 (over y, core), seq: 2 (over x), mp: 4 (over z).
Axes of the slice: x: 2, y: 2, z: 4, core: 2. Of those that a mesh axis runs over, the one named last changes fastest.
Arguments:
- queries: bfloat16 [4, 256, 2048], P('grp', 'seq', 'mp'), may hold values from -16 to 16
- d_out: bfloat16 [4, 256, 2048], P('grp', 'seq', 'mp'), may hold values from -6 to 6
- neighbour_kv: bfloat16 [4, 8, 128, 2, 2048], P('grp', 'seq', None, None, 'mp'), may hold values from -16 to 16
- target: int32 [4, 8], P('grp', 'seq'), may hold values from -1 to 7, as said below
- bias: float32 [16, 191], P('mp'), may hold values from -6 to 6
Outputs:
- attended: bfloat16 [4, 256, 2048], P('grp', 'seq', 'mp')
- d_query: bfloat16 [4, 256, 2048], P('grp', 'seq', 'mp')
- d_kv: bfloat16 [4, 8, 128, 2, 2048], P('grp', 'seq', None, None, 'mp')
- d_bias: float32 [16, 191], P('mp')
Inputs may be any that keep to these rules, and one draw needn't show every extreme that they name: `target`: in each group every entry 0..7 stands in exactly one slot and -1 marks an empty slot. The slots of one index of seq hold at most 2 entries e with the same e // 4, and some index reaches that; some index of seq holds 4 entries.
All inputs are finite; a program needn't handle non-finite values.
Results may differ from a plain program's by a relative error of at most 0.011.
Values may be sent and summed in bfloat16 or wider, within the bound.
A program may use at most 128 MiB of HBM per device.

v0:
```python
import jax
import jax.numpy as jnp
from jax import lax
from jax.sharding import PartitionSpec as P

STRETCH = 64
NB_LEN = 128


def passed_along(block, axis, distance):
    devices = range(lax.axis_size(axis))
    route = [(i - distance, i) for i in devices if i - distance in devices]
    return lax.ppermute(block, axis, route)


def bias_grid(lookup, row_count, col_count):
    head_num = lookup.shape[0]
    span = row_count + col_count
    padded = jnp.pad(lookup, ((0, 0), (0, 1)))
    flattened = jnp.tile(padded, (1, row_count))
    flattened = jnp.pad(flattened, ((0, 0), (0, row_count)))
    shaped = flattened.reshape(head_num, row_count, span + 1)[:, :, :col_count]
    return shaped[:, :, ::-1]


def bias_fold(grads):
    head_num, row_count, col_count = grads.shape
    turned = grads[:, :, ::-1]
    padded = jnp.pad(turned, ((0, 0), (0, 0), (0, row_count)))
    flattened = padded.reshape(head_num, row_count * (row_count + col_count))
    flattened = flattened[:, : row_count * (row_count + col_count - 1)]
    return jnp.sum(flattened.reshape(head_num, row_count, row_count + col_count - 1), axis=1)


def select_rows(picker, lookup):
    chosen = jnp.dot(
        picker.astype(lookup.dtype),
        lookup,
        preferred_element_type=jnp.float32,
        precision=lax.Precision.HIGHEST,
    )
    return chosen.astype(lookup.dtype)


def slot_places(target_row, owners, capacity, per_owner):
    is_used = target_row >= 0
    owner_of = jnp.where(is_used, target_row // per_owner, -1)
    positions = jnp.arange(target_row.shape[0])
    earlier = (
        (positions[None, :] < positions[:, None])
        & (owner_of[None, :] == owner_of[:, None])
        & is_used[None, :]
    )
    rank_of = jnp.sum(earlier.astype(jnp.int32), axis=1)
    match_owner = owner_of[None, :] == jnp.arange(owners)[:, None]
    match_rank = rank_of[None, :] == jnp.arange(capacity)[:, None]
    return match_owner[:, None, :] & match_rank[None, :, :] & is_used[None, None, :]


def local(queries, d_out, neighbour_kv, target, bias):
    tok_rows = queries.shape[1]
    width_dev = queries.shape[2]
    head_count = bias.shape[0]
    head_depth = width_dev // head_count
    stretch_count = tok_rows // STRETCH
    per_owner = 2 * stretch_count
    shard_count = lax.axis_size("seq")
    my_index = lax.axis_index("seq")
    group_size = min(shard_count, per_owner)
    capacity = (per_owner + group_size - 1) // group_size
    seq_stretches = min(2048, tok_rows * shard_count) // STRETCH
    scale_factor = head_depth ** (-0.5)
    bias_rows = bias_grid(bias, STRETCH, NB_LEN).transpose(1, 0, 2)
    q_rows = queries[0]
    g_rows = d_out[0]
    next_pair = passed_along(jnp.stack([q_rows[:STRETCH], g_rows[:STRETCH]]), "seq", -1)
    row_ids = jnp.arange(STRETCH)
    stretch_ids = my_index * stretch_count + jnp.arange(stretch_count)
    is_live = (row_ids[None, :] == 0) | ((stretch_ids[:, None] + 1) % seq_stretches != 0)
    live_rows = is_live.astype(jnp.float32)
    q_win = jnp.concatenate([q_rows, next_pair[0]])[STRETCH - 1 : STRETCH - 1 + tok_rows]
    q_win = q_win.reshape(stretch_count, STRETCH * width_dev)
    g_win = jnp.concatenate([g_rows, next_pair[1]])[STRETCH - 1 : STRETCH - 1 + tok_rows]
    g_win = g_win.reshape(stretch_count, STRETCH, width_dev) * is_live[:, :, None].astype(
        jnp.bfloat16
    )
    g_win = g_win.reshape(stretch_count, STRETCH * width_dev)
    my_targets = target[0]
    slot_count = my_targets.shape[0]
    send_map = slot_places(my_targets, shard_count, capacity, per_owner)
    id_buffer = jnp.sum(jnp.where(send_map, my_targets[None, None, :] + 1, 0), axis=2) - 1
    recv_ids = lax.all_to_all(id_buffer, "seq", split_axis=0, concat_axis=0, tiled=True)
    flat_ids = recv_ids.reshape(shard_count * capacity)
    has_entry = flat_ids >= 0
    local_entry = flat_ids - my_index * per_owner
    entry_pick = (local_entry[:, None] == jnp.arange(per_owner)[None, :]) & has_entry[:, None]
    stretch_pick = (local_entry[:, None] // 2 == jnp.arange(stretch_count)[None, :]) & has_entry[
        :, None
    ]
    back_pick = send_map.reshape(shard_count * capacity, slot_count)
    slot_pick = back_pick.T
    q_send = select_rows(stretch_pick, q_win).reshape(shard_count, capacity, STRETCH * width_dev)
    g_send = select_rows(stretch_pick, g_win).reshape(shard_count, capacity, STRETCH * width_dev)
    q_recv, g_recv = (
        lax.all_to_all(q_send, "seq", split_axis=0, concat_axis=0, tiled=True),
        lax.all_to_all(g_send, "seq", split_axis=0, concat_axis=0, tiled=True),
    )
    q_slots = select_rows(slot_pick, q_recv.reshape(shard_count * capacity, -1))
    q_slots = q_slots.reshape(slot_count, STRETCH, head_count, head_depth)
    stored = neighbour_kv[0]
    key_rows = stored[:, :, 0].reshape(slot_count, NB_LEN, head_count, head_depth)
    value_rows = stored[:, :, 1].reshape(slot_count, NB_LEN, head_count, head_depth)
    scores = jnp.einsum("sihd,sjhd->sihj", q_slots, key_rows, preferred_element_type=jnp.float32)
    scores = scores * scale_factor + bias_rows[None]
    peak_val = jnp.max(scores, axis=-1)
    weights = jnp.exp(scores - peak_val[..., None])
    row_total = jnp.sum(weights, axis=-1)
    partial_value = jnp.einsum(
        "sihj,sjhd->sihd",
        weights.astype(jnp.bfloat16),
        value_rows,
        preferred_element_type=jnp.float32,
    )
    part_send = select_rows(back_pick, partial_value.reshape(slot_count, -1)).reshape(
        shard_count, capacity, -1
    )
    peak_send = select_rows(back_pick, peak_val.reshape(slot_count, -1)).reshape(
        shard_count, capacity, -1
    )
    total_send = select_rows(back_pick, row_total.reshape(slot_count, -1)).reshape(
        shard_count, capacity, -1
    )
    part_recv, peak_recv, total_recv = (
        lax.all_to_all(part_send, "seq", split_axis=0, concat_axis=0, tiled=True),
        lax.all_to_all(peak_send, "seq", split_axis=0, concat_axis=0, tiled=True),
        lax.all_to_all(total_send, "seq", split_axis=0, concat_axis=0, tiled=True),
    )
    entry_back = entry_pick.T
    parts_own = select_rows(entry_back, part_recv.reshape(shard_count * capacity, -1))
    parts_own = parts_own.reshape(stretch_count, 2, STRETCH, head_count, head_depth)
    peaks_own = select_rows(entry_back, peak_recv.reshape(shard_count * capacity, -1))
    peaks_own = peaks_own.reshape(stretch_count, 2, STRETCH, head_count)
    totals_own = select_rows(entry_back, total_recv.reshape(shard_count * capacity, -1))
    totals_own = totals_own.reshape(stretch_count, 2, STRETCH, head_count)
    top_peak = jnp.max(peaks_own, axis=1)
    factor = jnp.exp(peaks_own - top_peak[:, None])
    denominator = jnp.sum(factor * totals_own, axis=1)
    combined = jnp.sum(factor[..., None] * parts_own, axis=1) / denominator[..., None]
    combined = combined * live_rows[:, :, None, None]
    att_win = combined.astype(jnp.bfloat16).reshape(tok_rows, width_dev)
    log_total = top_peak + jnp.log(denominator)
    g_wide = g_win.reshape(stretch_count, STRETCH, head_count, head_depth).astype(jnp.float32)
    inner_dot = jnp.sum(g_wide * combined, axis=-1)
    row_stats = jnp.repeat(jnp.stack([log_total, inner_dot], axis=1), 2, axis=0)
    stats_send = select_rows(entry_pick, row_stats.reshape(per_owner, -1)).reshape(
        shard_count, capacity, -1
    )
    stats_recv = lax.all_to_all(stats_send, "seq", split_axis=0, concat_axis=0, tiled=True)
    g_slots = select_rows(slot_pick, g_recv.reshape(shard_count * capacity, -1))
    g_slots = g_slots.reshape(slot_count, STRETCH, head_count, head_depth)
    stats_slots = select_rows(slot_pick, stats_recv.reshape(shard_count * capacity, -1))
    stats_slots = stats_slots.reshape(slot_count, 2, STRETCH, head_count)
    prob_full = jnp.exp(scores - stats_slots[:, 0][..., None])
    prob_low = prob_full.astype(jnp.bfloat16)
    grad_values = jnp.einsum(
        "sihj,sihd->sjhd", prob_low, g_slots, preferred_element_type=jnp.float32
    )
    grad_prob = jnp.einsum(
        "sihd,sjhd->sihj", g_slots, value_rows, preferred_element_type=jnp.float32
    )
    grad_scores = prob_full * (grad_prob - stats_slots[:, 1][..., None])
    scores_low = grad_scores.astype(jnp.bfloat16)
    grad_rows = (
        jnp.einsum("sihj,sjhd->sihd", scores_low, key_rows, preferred_element_type=jnp.float32)
        * scale_factor
    )
    grad_keys = (
        jnp.einsum("sihj,sihd->sjhd", scores_low, q_slots, preferred_element_type=jnp.float32)
        * scale_factor
    )
    d_kv = jnp.stack(
        [
            grad_keys.reshape(slot_count, NB_LEN, width_dev),
            grad_values.reshape(slot_count, NB_LEN, width_dev),
        ],
        axis=2,
    ).astype(jnp.bfloat16)
    bias_part = bias_fold(jnp.sum(grad_scores, axis=0).transpose(1, 0, 2))
    rows_send = select_rows(back_pick, grad_rows.reshape(slot_count, -1)).reshape(
        shard_count, capacity, -1
    )
    rows_recv = lax.all_to_all(rows_send, "seq", split_axis=0, concat_axis=0, tiled=True)
    grad_entries = select_rows(entry_back, rows_recv.reshape(shard_count * capacity, -1))
    grad_entries = grad_entries.reshape(stretch_count, 2, STRETCH * width_dev)
    grad_win = (
        (grad_entries[:, 0] + grad_entries[:, 1]).astype(jnp.bfloat16).reshape(tok_rows, width_dev)
    )
    both_before = passed_along(
        jnp.stack([att_win[tok_rows - STRETCH :], grad_win[tok_rows - STRETCH :]]), "seq", 1
    )
    att_before = both_before[0]
    grad_before = both_before[1]
    attended = jnp.concatenate([att_before[1:], att_win[: tok_rows - STRETCH + 1]])
    d_query = jnp.concatenate([grad_before[1:], grad_win[: tok_rows - STRETCH + 1]])
    raw_sum = lax.psum(bias_part, ("grp", "seq"))
    squares = lax.psum(jnp.sum(raw_sum * raw_sum), "mp")
    d_bias = raw_sum * jnp.minimum(1.0, 1.0 / jnp.sqrt(squares + 1e-12))
    return (attended[None], d_query[None], d_kv[None], d_bias)


def solution(mesh):
    in_specs = (
        P("grp", "seq", "mp"),
        P("grp", "seq", "mp"),
        P("grp", "seq", None, None, "mp"),
        P("grp", "seq"),
        P("mp", None),
    )
    out_specs = (
        P("grp", "seq", "mp"),
        P("grp", "seq", "mp"),
        P("grp", "seq", None, None, "mp"),
        P("mp", None),
    )
    return jax.shard_map(local, mesh=mesh, in_specs=in_specs, out_specs=out_specs, check_vma=False)
```

profile of v0, /device:TPU:0, one launch (start us, length us, event | category | flops | bytes accessed | tf_op | source)
XLA Modules:
  0.0 128.0 jit_solution(2037789528127061619)
XLA Ops:
  2.3 1.3 %collective-permute-start = (bf16[2,64,512]{2,1,0:T(8,128)(2,1)S(1)}, bf16[2,64,512]{2,1,0:T(8,128)(2,1)S(1)}, u32[]{:S(2)}, u32[]{:S(2)}) collective-permute-start(bf16[2,64,512]{2,1,0:T(8,128)(2,1)S(1)} %pad_maximum_fusion.3), channel_id=1, source_target_pairs={{4,0},{5,1},{6,2},{7,3},{12,8},{13,9},{14,10},{15,11},{20,16},{21,... | collective-permute-start | bytes 393224 | tf_op jit(solution)/shard_map/ppermute | solution.py:13
  7.2 4.2 %all-to-all-start = ((s32[2,1,2]{2,1,0:T(1,128)}), s32[2,1,2]{2,1,0:T(1,128)S(1)}, u32[]{:S(2)}, u32[]{:S(2)}) async-start(s32[2,1,2]{2,1,0:T(1,128)} %bitcast.4), calls=%async_computation | async-start | bytes 2048 | tf_op jit(solution)/shard_map/all_to_all | solution.py:92
  11.5 2.5 %copy.123 = bf16[1,4,128,2,512]{2,4,1,3,0:T(8,128)(2,1)S(1)} copy(bf16[1,4,128,2,512]{4,3,2,1,0:T(2,128)(2,1)} %param.7) | data formatting | bytes 2097152 | tf_op args[2]
  18.1 1.2 fusion.58
  21.6 3.4 %all-to-all-start.1 = ((bf16[2,2,32768]{2,1,0:T(2,128)(2,1)}), bf16[2,2,32768]{2,1,0:T(2,128)(2,1)S(1)}, u32[]{:S(2)}, u32[]{:S(2)}) async-start(bf16[2,2,32768]{2,1,0:T(2,128)(2,1)} %reshape.529), calls=%async_computation.1 | async-start | bytes 524288 | tf_op jit(solution)/shard_map/all_to_all | solution.py:105
  26.3 4.5 %all-to-all-done.1 = bf16[2,2,32768]{2,1,0:T(2,128)(2,1)S(1)} async-done(((bf16[2,2,32768]{2,1,0:T(2,128)(2,1)}), bf16[2,2,32768]{2,1,0:T(2,128)(2,1)S(1)}, u32[]{:S(2)}, u32[]{:S(2)}) %all-to-all-start.1) | async-done | bytes 262176 | tf_op jit(solution)/shard_map/all_to_all | solution.py:105
  30.7 3.4 %all-to-all-start.6 = ((bf16[2,2,32768]{2,1,0:T(2,128)(2,1)}), bf16[2,2,32768]{2,1,0:T(2,128)(2,1)S(1)}, u32[]{:S(2)}, u32[]{:S(2)}) async-start(bf16[2,2,32768]{2,1,0:T(2,128)(2,1)} %reshape.541), calls=%async_computation.6 | async-start | bytes 524288 | tf_op jit(solution)/shard_map/all_to_all | solution.py:106
  37.1 1.6 %fusion.64 = f32[2,2,32768]{2,1,0:T(2,128)} fusion(pred[2,2,4]{2,1,0:T(4,128)(4,1)S(1)} %get-tuple-element.12, f32[4,32768,1]{1,0,2:T(4,128)S(1)} %reshape.551), kind=kOutput, calls=%fused_computation.137 | convolution fusion | flops 6291456 | bytes 1048592 | tf_op jit(solution)/shard_map/dot_general | solution.py:36
  39.8 3.3 %all-to-all-start.2 = ((f32[2,2,256]{2,1,0:T(2,128)}), f32[2,2,256]{2,1,0:T(2,128)S(1)}, u32[]{:S(2)}, u32[]{:S(2)}) async-start(f32[2,2,256]{2,1,0:T(2,128)} %fusion.63), calls=%async_computation.2 | async-start | bytes 8192 | tf_op jit(solution)/shard_map/all_to_all | solution.py:135
  43.8 3.1 %all-to-all-done.2 = f32[2,2,256]{2,1,0:T(2,128)S(1)} async-done(((f32[2,2,256]{2,1,0:T(2,128)}), f32[2,2,256]{2,1,0:T(2,128)S(1)}, u32[]{:S(2)}, u32[]{:S(2)}) %all-to-all-start.2) | async-done | bytes 4128 | tf_op jit(solution)/shard_map/all_to_all | solution.py:135
  46.9 3.2 %all-to-all-start.4 = ((f32[2,2,256]{2,1,0:T(2,128)}), f32[2,2,256]{2,1,0:T(2,128)S(1)}, u32[]{:S(2)}, u32[]{:S(2)}) async-start(f32[2,2,256]{2,1,0:T(2,128)} %fusion.65), calls=%async_computation.4 | async-start | bytes 8192 | tf_op jit(solution)/shard_map/all_to_all | solution.py:136
  51.1 2.8 %all-to-all-done.4 = f32[2,2,256]{2,1,0:T(2,128)S(1)} async-done(((f32[2,2,256]{2,1,0:T(2,128)}), f32[2,2,256]{2,1,0:T(2,128)S(1)}, u32[]{:S(2)}, u32[]{:S(2)}) %all-to-all-start.4) | async-done | bytes 4128 | tf_op jit(solution)/shard_map/all_to_all | solution.py:136
  53.9 3.5 %all-to-all-start.3 = ((f32[2,2,32768]{2,1,0:T(2,128)}), f32[2,2,32768]{2,1,0:T(2,128)S(1)}, u32[]{:S(2)}, u32[]{:S(2)}) async-start(f32[2,2,32768]{2,1,0:T(2,128)} %fusion.64), calls=%async_computation.3 | async-start | bytes 1048576 | tf_op jit(solution)/shard_map/all_to_all | solution.py:134
  59.1 4.9 %all-to-all-done.3 = f32[2,2,32768]{2,1,0:T(2,128)S(1)} async-done(((f32[2,2,32768]{2,1,0:T(2,128)}), f32[2,2,32768]{2,1,0:T(2,128)S(1)}, u32[]{:S(2)}, u32[]{:S(2)}) %all-to-all-start.3) | async-done | bytes 524320 | tf_op jit(solution)/shard_map/all_to_all | solution.py:134
  64.5 2.4 %fusion.8 = f32[2,64,4,128]{3,2,1,0:T(4,128)S(1)} fusion(f32[64,4,128,4,1]{2,3,1,0,4:T(4,128)S(1)} %bitcast.168, f32[2,2,64,4]{1,3,2,0:T(4,128)S(1)} %copy.128, pred[4]{0:T(512)(128)(4,1)S(1)} %copy-done.13, s32[2,2]{1,0:T(2,128)} %copy-done.8, s32[4]{0:T(128)} %copy-done.10), kind=kOutput, calls=%fused_computation.19 | convolution fusion | flops 6488096 | bytes 790564 | tf_op jit(solution)/shard_map/dot_general | solution.py:36
  68.9 3.4 %all-to-all-start.5 = ((f32[2,2,512]{2,1,0:T(2,128)}), f32[2,2,512]{2,1,0:T(2,128)S(1)}, u32[]{:S(2)}, u32[]{:S(2)}) async-start(f32[2,2,512]{2,1,0:T(2,128)} %fusion.30), calls=%async_computation.5 | async-start | bytes 16384 | tf_op jit(solution)/shard_map/all_to_all | solution.py:158
  72.4 3.5 %all-to-all-done.5 = f32[2,2,512]{2,1,0:T(2,128)S(1)} async-done(((f32[2,2,512]{2,1,0:T(2,128)}), f32[2,2,512]{2,1,0:T(2,128)S(1)}, u32[]{:S(2)}, u32[]{:S(2)}) %all-to-all-start.5) | async-done | bytes 8224 | tf_op jit(solution)/shard_map/all_to_all | solution.py:158
  78.7 1.6 %fusion.66 = f32[2,2,32768]{2,1,0:T(2,128)} fusion(pred[2,2,4]{2,1,0:T(4,128)(4,1)S(1)} %get-tuple-element.12, f32[4,32768,1]{1,0,2:T(4,128)S(1)} %reshape.559), kind=kOutput, calls=%fused_computation.139 | convolution fusion | flops 6291456 | bytes 1048592 | tf_op jit(solution)/shard_map/dot_general | solution.py:36
  80.3 4.2 %all-to-all-start.7 = ((f32[2,2,32768]{2,1,0:T(2,128)}), f32[2,2,32768]{2,1,0:T(2,128)}, u32[]{:S(2)}, u32[]{:S(2)}) async-start(f32[2,2,32768]{2,1,0:T(2,128)} %fusion.66), calls=%async_computation.7 | async-start | bytes 1048576 | tf_op jit(solution)/shard_map/all_to_all | solution.py:192
  85.1 14.2 %psum.14 = f32[4,191]{1,0:T(4,128)S(1)} all-reduce(f32[4,191]{1,0:T(4,128)S(1)} %reduce_sum.88), channel_id=1, replica_groups=mesh['grp'=4,'seq'=2,'mp'=4] {'grp','seq'}, use_global_device_ids=true, to_apply=%region_10.11 | all-reduce | flops 764 | bytes 6112 | tf_op jit(solution)/shard_map/psum | solution.py:205
  100.2 13.2 %psum.15 = f32[]{:T(128)} all-reduce(f32[]{:T(128)} %multiply_reduce_fusion.1), channel_id=1, replica_groups=mesh['grp'=4,'seq'=2,'mp'=4] {'mp'}, use_global_device_ids=true, to_apply=%region_12.13 | all-reduce | flops 1 | bytes 8 | tf_op jit(solution)/shard_map/psum | solution.py:206
  116.4 1.5 %reshape.560 = f32[4,32768,1]{1,0,2:T(4,128)S(1)} reshape(f32[2,2,32768]{2,1,0:T(2,128)} %all-to-all-done.7) | data formatting | bytes 1048576 | tf_op jit(solution)/shard_map/reshape | solution.py:193
  120.3 3.0 %collective-permute-start.1 = (bf16[2,64,512]{2,1,0:T(8,128)(2,1)S(1)}, bf16[2,64,512]{2,1,0:T(8,128)(2,1)S(1)}, u32[]{:S(2)}, u32[]{:S(2)}) collective-permute-start(bf16[2,64,512]{2,1,0:T(8,128)(2,1)S(1)} %pad_maximum_fusion.4), channel_id=1, source_target_pairs={{0,4},{1,5},{2,6},{3,7},{8,12},{9,13},{10,14},{11,15},{16,20},{17,... | collective-permute-start | bytes 393224 | tf_op jit(solution)/shard_map/ppermute | solution.py:13
  123.3 3.2 %pad_maximum_fusion = bf16[1,4,128,2,512]{4,3,2,1,0:T(2,128)(2,1)} fusion(bf16[1,4,128,1,512]{4,3,2,1,0:T(2,128)(2,1)S(1)} %copy.147, bf16[1,4,128,1,512]{4,3,2,1,0:T(2,128)(2,1)S(1)} %copy.146), kind=kLoop, calls=%fused_computation.22 | loop fusion | flops 2097152 | bytes 2097152 | tf_op jit(solution)/shard_map/stack | solution.py:181
  (159 shorter events, 32.8 us)
Async XLA Ops:
  2.3 17.7 %collective-permute-start = (bf16[2,64,512]{2,1,0:T(8,128)(2,1)S(1)}, bf16[2,64,512]{2,1,0:T(8,128)(2,1)S(1)}, u32[]{:S(2)}, u32[]{:S(2)}) collective-permute-start(bf16[2,64,512]{2,1,0:T(8,128)(2,1)S(1)} %pad_maximum_fusion.3), channel_id=1, source_target_pairs={{4,0},{5,1},{6,2},{7,3},{12,8},{13,9},{14,10},{15,11},{20,16},{21,... | collective-permute-start | bytes 393224 | tf_op jit(solution)/shard_map/ppermute | solution.py:13
  7.2 10.4 %all-to-all-start = ((s32[2,1,2]{2,1,0:T(1,128)}), s32[2,1,2]{2,1,0:T(1,128)S(1)}, u32[]{:S(2)}, u32[]{:S(2)}) async-start(s32[2,1,2]{2,1,0:T(1,128)} %bitcast.4), calls=%async_computation | async-start | bytes 2048 | tf_op jit(solution)/shard_map/all_to_all | solution.py:92
  11.4 46.5 %copy-start.8 = (s32[2,2]{1,0:T(2,128)}, s32[2,2]{1,0:T(2,128)S(1)}, u32[]{:S(2)}) copy-start(s32[2,2]{1,0:T(2,128)S(1)} %multiply_add_fusion) | copy-start | bytes 52
  14.9 5.2 %copy-start = (bf16[1,128,512]{2,1,0:T(8,128)(2,1)S(1)}, bf16[1,128,512]{2,1,0:T(8,128)(2,1)}, u32[]{:S(2)}) copy-start(bf16[1,128,512]{2,1,0:T(8,128)(2,1)} %param.6) | copy-start | bytes 393220
  15.3 5.0 %copy-start.1 = (bf16[1,128,512]{2,1,0:T(8,128)(2,1)S(1)}, bf16[1,128,512]{2,1,0:T(8,128)(2,1)}, u32[]{:S(2)}) copy-start(bf16[1,128,512]{2,1,0:T(8,128)(2,1)} %param.5) | copy-start | bytes 393220
  16.0 4.4 %copy-start.3 = (bf16[2,64]{1,0:T(2,128)(2,1)}, bf16[2,64]{1,0:T(2,128)(2,1)S(1)}, u32[]{:S(2)}) copy-start(bf16[2,64]{1,0:T(2,128)(2,1)S(1)} %get-tuple-element.24) | copy-start | bytes 772
  19.4 38.5 %copy-start.10 = (s32[4]{0:T(128)}, s32[4]{0:T(128)S(1)}, u32[]{:S(2)}) copy-start(s32[4]{0:T(128)S(1)} %sub.77) | copy-start | bytes 52
  19.6 38.4 %copy-start.12 = (pred[4]{0:T(512)(128)(4,1)}, pred[4]{0:T(512)(128)(4,1)S(1)}, u32[]{:S(2)}) copy-start(pred[4]{0:T(512)(128)(4,1)S(1)} %ge.32) | copy-start | bytes 16
  21.6 9.1 %all-to-all-start.1 = ((bf16[2,2,32768]{2,1,0:T(2,128)(2,1)}), bf16[2,2,32768]{2,1,0:T(2,128)(2,1)S(1)}, u32[]{:S(2)}, u32[]{:S(2)}) async-start(bf16[2,2,32768]{2,1,0:T(2,128)(2,1)} %reshape.529), calls=%async_computation.1 | async-start | bytes 524288 | tf_op jit(solution)/shard_map/all_to_all | solution.py:105
  30.7 9.1 %all-to-all-start.6 = ((bf16[2,2,32768]{2,1,0:T(2,128)(2,1)}), bf16[2,2,32768]{2,1,0:T(2,128)(2,1)S(1)}, u32[]{:S(2)}, u32[]{:S(2)}) async-start(bf16[2,2,32768]{2,1,0:T(2,128)(2,1)} %reshape.541), calls=%async_computation.6 | async-start | bytes 524288 | tf_op jit(solution)/shard_map/all_to_all | solution.py:106
  39.8 7.1 %all-to-all-start.2 = ((f32[2,2,256]{2,1,0:T(2,128)}), f32[2,2,256]{2,1,0:T(2,128)S(1)}, u32[]{:S(2)}, u32[]{:S(2)}) async-start(f32[2,2,256]{2,1,0:T(2,128)} %fusion.63), calls=%async_computation.2 | async-start | bytes 8192 | tf_op jit(solution)/shard_map/all_to_all | solution.py:135
  46.9 7.0 %all-to-all-start.4 = ((f32[2,2,256]{2,1,0:T(2,128)}), f32[2,2,256]{2,1,0:T(2,128)S(1)}, u32[]{:S(2)}, u32[]{:S(2)}) async-start(f32[2,2,256]{2,1,0:T(2,128)} %fusion.65), calls=%async_computation.4 | async-start | bytes 8192 | tf_op jit(solution)/shard_map/all_to_all | solution.py:136
  53.9 10.1 %all-to-all-start.3 = ((f32[2,2,32768]{2,1,0:T(2,128)}), f32[2,2,32768]{2,1,0:T(2,128)S(1)}, u32[]{:S(2)}, u32[]{:S(2)}) async-start(f32[2,2,32768]{2,1,0:T(2,128)} %fusion.64), calls=%async_computation.3 | async-start | bytes 1048576 | tf_op jit(solution)/shard_map/all_to_all | solution.py:134
  58.2 6.2 %copy-start.13 = (pred[4]{0:T(512)(128)(4,1)S(1)}, pred[4]{0:T(512)(128)(4,1)}, u32[]{:S(2)}) copy-start(pred[4]{0:T(512)(128)(4,1)} %copy-done.12) | copy-start | bytes 16
  64.4 2.5 %copy-start.2 = (f32[2,64,4]{2,1,0:T(8,128)S(1)}, f32[2,64,4]{2,1,0:T(8,128)}, u32[]{:S(2)}) copy-start(f32[2,64,4]{2,1,0:T(8,128)} %copy.133) | copy-start | bytes 6148
  64.4 2.5 %copy-start.4 = (bf16[2,64]{1,0:T(2,128)(2,1)S(1)}, bf16[2,64]{1,0:T(2,128)(2,1)}, u32[]{:S(2)}) copy-start(bf16[2,64]{1,0:T(2,128)(2,1)} %copy-done.3) | copy-start | bytes 772
  66.9 5.4 %copy-start.16 = (f32[128]{0:T(128)S(1)}, f32[128]{0:T(128)}, u32[]{:S(2)}) copy-start(f32[128]{0:T(128)} %or_convert_fusion.2) | copy-start | bytes 1540
  67.6 8.7 %copy-start.15 = (pred[4,4]{1,0:T(4,128)(4,1)S(1)}, pred[4,4]{1,0:T(4,128)(4,1)}, u32[]{:S(2)}) copy-start(pred[4,4]{1,0:T(4,128)(4,1)} %and.168) | copy-start | bytes 52
  68.9 7.0 %all-to-all-start.5 = ((f32[2,2,512]{2,1,0:T(2,128)}), f32[2,2,512]{2,1,0:T(2,128)S(1)}, u32[]{:S(2)}, u32[]{:S(2)}) async-start(f32[2,2,512]{2,1,0:T(2,128)} %fusion.30), calls=%async_computation.5 | async-start | bytes 16384 | tf_op jit(solution)/shard_map/all_to_all | solution.py:158
  80.3 36.1 %all-to-all-start.7 = ((f32[2,2,32768]{2,1,0:T(2,128)}), f32[2,2,32768]{2,1,0:T(2,128)}, u32[]{:S(2)}, u32[]{:S(2)}) async-start(f32[2,2,32768]{2,1,0:T(2,128)} %fusion.66), calls=%async_computation.7 | async-start | bytes 1048576 | tf_op jit(solution)/shard_map/all_to_all | solution.py:192
  114.3 3.7 %copy-start.9 = (s32[2,2]{1,0:T(2,128)S(1)}, s32[2,2]{1,0:T(2,128)}, u32[]{:S(2)}) copy-start(s32[2,2]{1,0:T(2,128)} %copy-done.8) | copy-start | bytes 52
  114.3 3.7 %copy-start.11 = (s32[4]{0:T(128)S(1)}, s32[4]{0:T(128)}, u32[]{:S(2)}) copy-start(s32[4]{0:T(128)} %copy-done.10) | copy-start | bytes 52
  114.3 3.7 %copy-start.14 = (pred[4]{0:T(512)(128)(4,1)S(1)}, pred[4]{0:T(512)(128)(4,1)}, u32[]{:S(2)}) copy-start(pred[4]{0:T(512)(128)(4,1)} %copy-done.12) | copy-start | bytes 16
  120.3 6.4 %collective-permute-start.1 = (bf16[2,64,512]{2,1,0:T(8,128)(2,1)S(1)}, bf16[2,64,512]{2,1,0:T(8,128)(2,1)S(1)}, u32[]{:S(2)}, u32[]{:S(2)}) collective-permute-start(bf16[2,64,512]{2,1,0:T(8,128)(2,1)S(1)} %pad_maximum_fusion.4), channel_id=1, source_target_pairs={{0,4},{1,5},{2,6},{3,7},{8,12},{9,13},{10,14},{11,15},{16,20},{17,... | collective-permute-start | bytes 393224 | tf_op jit(solution)/shard_map/ppermute | solution.py:13
  (4 other events, 5.4 us)
where the time goes:
time: 129 us; the launch traced here: 128 us
  starting transfers between devices  33 us (26%)
  blocking collectives  27.3 us (21%)
  local copies, waits for them, and re-layouts  19 us (15%)
  waiting for transfers between devices  18.6 us (14%)
  other arithmetic  14.2 us (11%)
  matrix products  13.7 us (11%)
  between operations  2.11 us (2%)
    psum x1, blocking collectives, local(): raw_sum = lax.psum(bias_part, ('grp', 'seq'))  14.2 us
    psum x1, blocking collectives, local(): squares = lax.psum(jnp.sum(raw_sum * raw_sum), 'mp')  13.2 us
    dot_general x14, matrix products, select_rows(): jnp.dot(picker.astype(lookup.dtype), lookup, preferred_element_type=jnp.f...  11.1 us
    all_to_all x1, waiting for transfers between devices, local(): lax.all_to_all(part_send, 'seq', split_axis=0, concat_axis=0, tiled=True)  4.85 us
    all_to_all x1, waiting for transfers between devices, local(): lax.all_to_all(q_send, 'seq', split_axis=0, concat_axis=0, tiled=True)  4.48 us
    ppermute x2, starting transfers between devices, passed_along(): return lax.ppermute(block, axis, route)  4.34 us
    all_to_all x1, starting transfers between devices, local(): lax.all_to_all(id_buffer, 'seq', split_axis=0, concat_axis=0, tiled=True)  4.21 us
    all_to_all x1, starting transfers between devices, local(): lax.all_to_all(rows_send, 'seq', split_axis=0, concat_axis=0, tiled=True)  4.2 us
  transfers between devices with their start and end apart: 10, of which 5 were waited for; matrix products, arithmetic and copies ran while one was open for 23% of the time, Pallas kernels for 0%

commit v1 on v0

--- a/solution.py
+++ b/solution.py
@@ -1,6 +1,8 @@
 import jax
 import jax.numpy as jnp
 from jax import lax
+from jax.experimental import pallas as pl
+from jax.experimental.pallas import tpu as pltpu
 from jax.sharding import PartitionSpec as P
 
 STRETCH = 64
@@ -57,7 +59,7 @@
     return match_owner[:, None, :] & match_rank[None, :, :] & is_used[None, None, :]
 
 
-def local(queries, d_out, neighbour_kv, target, bias):
+def shard_exchange(queries, d_out, neighbour_kv, target, bias):
     tok_rows = queries.shape[1]
     width_dev = queries.shape[2]
     head_count = bias.shape[0]
@@ -208,6 +210,289 @@
     return (attended[None], d_query[None], d_kv[None], d_bias)
 
 
+WIDE = 2 * NB_LEN
+HALF = 256
+MESH = pl.DeviceIdType.MESH
+
+
+def dot(a, b, contract=((1,), (0,))):
+    return lax.dot_general(a, b, (contract, ((), ())), preferred_element_type=jnp.float32)
+
+
+def iota(shape, axis):
+    return lax.broadcasted_iota(jnp.int32, shape, axis)
+
+
+def pair_kernel(
+    q_ref, g_ref, kv_ref, target_ref, bias_ref,
+    att_ref, dq_ref, dkv_ref, dbias_ref,
+    q_peer, g_peer, windows, weights, cotangents, mixed, rows_own, rows_send, rows_recv,
+    stat_send, stat_recv, raw_all, norm_all,
+    in_send, in_recv, stat_sems, row_send_sems, row_recv_sems,
+    raw_send_sems, raw_recv_sems, norm_send_sems, norm_recv_sems,
+):
+    heads = bias_ref.shape[0]
+    slots = kv_ref.shape[0]
+    tok = q_ref.shape[0]
+    depth = kv_ref.shape[-1]
+    groups, mps = lax.axis_size("grp"), lax.axis_size("mp")
+    plane = 2 * groups
+    scale = depth ** (-0.5)
+    grp, seq, mp = lax.axis_index("grp"), lax.axis_index("seq"), lax.axis_index("mp")
+    here = grp * 2 + seq
+    peer = {"seq": 1 - seq}
+
+    def plane_at(step):
+        there = lax.rem(here + step, plane)
+        return {"grp": there // 2, "seq": there % 2}
+
+    def mp_at(step):
+        return {"mp": lax.rem(mp + step, mps)}
+
+    barrier = pltpu.get_barrier_semaphore()
+    for step in range(1, plane):
+        pl.semaphore_signal(barrier, inc=1, device_id=plane_at(step), device_id_type=MESH)
+    for step in range(1, mps):
+        pl.semaphore_signal(barrier, inc=1, device_id=mp_at(step), device_id_type=MESH)
+    pl.semaphore_wait(barrier, plane - 1 + mps - 1)
+
+    def send(src, dst, send_sem, recv_sem, device):
+        copy = pltpu.make_async_remote_copy(
+            src_ref=src, dst_ref=dst, send_sem=send_sem, recv_sem=recv_sem,
+            device_id=device, device_id_type=MESH,
+        )
+        copy.start()
+        return copy
+
+    in_copies = []
+    for h in range(heads):
+        cols = pl.ds(h * depth, depth)
+        in_copies.append((
+            send(q_ref.at[:, cols], q_peer.at[h], in_send.at[2 * h], in_recv.at[2 * h], peer),
+            send(g_ref.at[:, cols], g_peer.at[h], in_send.at[2 * h + 1], in_recv.at[2 * h + 1], peer),
+        ))
+
+    entries = [target_ref[0, r] for r in range(slots)]
+    firsts = [(STRETCH - 1) + STRETCH * (e // 2) for e in entries]
+
+    def token_of(axis, shape):
+        place = iota(shape, axis)
+        return jnp.where(place < tok, tok * seq + place, tok * (1 - seq) + place - tok)
+
+    def one_hot(flags):
+        return jnp.where(flags, 1.0, 0.0).astype(jnp.bfloat16)
+
+    gather = jnp.concatenate(
+        [
+            one_hot(token_of(1, (STRETCH, 2 * tok)) == iota((STRETCH, 2 * tok), 0) + firsts[r])
+            for r in range(slots)
+        ],
+        axis=0,
+    )
+    odd = iota((STRETCH, WIDE), 1) % 2 == 1
+    lane = iota((STRETCH, 128), 1)
+    table = jnp.zeros((STRETCH, 128), jnp.float32)
+    for h in range(heads):
+        wide = jnp.broadcast_to(bias_ref[h : h + 1, :], (STRETCH, 2 * WIDE))
+        grid = pltpu.roll(wide, 2 * WIDE - 126, 1, stride=2, stride_axis=0)[:, :WIDE]
+        grid = jnp.where(odd, -1e30, grid)
+        cols = pl.ds(h * depth, depth)
+        mine = jnp.concatenate([q_ref[:, cols], g_ref[:, cols]], axis=1)
+        for copy in in_copies[h]:
+            copy.wait_recv()
+        other = jnp.concatenate([q_peer[h], g_peer[h]], axis=1)
+        picked = dot(gather, jnp.concatenate([mine, other], axis=0)).astype(jnp.bfloat16)
+        for r in range(slots):
+            rows = picked[r * STRETCH : (r + 1) * STRETCH]
+            both = jnp.concatenate([rows[:, :depth], rows[:, depth:]], axis=0)
+            windows[h, r] = both
+            prod = dot(both, kv_ref[r, h], ((1,), (1,)))
+            scores = prod[:STRETCH] * scale + grid
+            grad_prob = prod[STRETCH:]
+            peak = jnp.max(scores, axis=1, keepdims=True)
+            expd = jnp.exp(scores - peak)
+            total = jnp.sum(expd, axis=1, keepdims=True)
+            expd = pltpu.roll(expd, 1, 1)
+            inner = jnp.sum(expd * grad_prob, axis=1, keepdims=True)
+            weights[h, r] = expd
+            cotangents[h, r] = grad_prob
+            base = entries[r] * heads + h
+            table = jnp.where(lane == base, peak, table)
+            table = jnp.where(lane == base + 32, total, table)
+            table = jnp.where(lane == base + 64, inner, table)
+    stat_send[...] = table
+    stat_copy = send(stat_send, stat_recv, stat_sems.at[0], stat_sems.at[1], peer)
+    stat_copy.wait_recv()
+    table = table + stat_recv[...]
+
+    def partner(x):
+        return jnp.where((lane // heads) % 2 == 0, pltpu.roll(x, 128 - heads, 1), pltpu.roll(x, heads, 1))
+
+    total = pltpu.roll(table, 96, 1)
+    inner = pltpu.roll(table, 64, 1)
+    other_peak = partner(table)
+    top = jnp.maximum(table, other_peak)
+    mine_f, other_f = jnp.exp(table - top), jnp.exp(other_peak - top)
+    denominator = mine_f * total + other_f * partner(total)
+    inner = (mine_f * inner + other_f * partner(inner)) / denominator
+    norm = mine_f / denominator
+
+    for h in range(heads):
+        bias_sum = jnp.zeros((STRETCH, WIDE), jnp.float32)
+        for r in range(slots):
+            at = lane == entries[r] * heads + h
+            factor = jnp.sum(jnp.where(at, norm, 0.0), axis=1, keepdims=True)
+            shift = jnp.sum(jnp.where(at, inner, 0.0), axis=1, keepdims=True)
+            prob = weights[h, r] * factor
+            grad = prob * (cotangents[h, r] - shift)
+            bias_sum = bias_sum + grad
+            mixed[h, r, :STRETCH] = pltpu.roll(grad, WIDE - 1, 1).astype(jnp.bfloat16)
+            mixed[h, r, STRETCH:] = prob.astype(jnp.bfloat16)
+        folded = jnp.concatenate([bias_sum, jnp.zeros_like(bias_sum)], axis=1)
+        half = STRETCH // 2
+        while half >= 8:
+            folded = pltpu.roll(folded[:half], 2 * half, 1) + folded[half:]
+            half //= 2
+        row8 = iota((8, 2 * WIDE), 0)
+        for bit in (4, 2, 1):
+            folded = jnp.where((row8 // bit) % 2 == 0, pltpu.roll(folded, 2 * bit, 1), folded)
+        folded = jnp.sum(folded, axis=0, keepdims=True)
+        if h == 0:
+            stacked = jnp.zeros((8, 2 * WIDE), jnp.float32)
+        stacked = jnp.where(row8 == h, folded, stacked)
+    unmix = jnp.where(
+        iota((2 * WIDE, WIDE), 0) == 381 - 2 * iota((2 * WIDE, WIDE), 1), 1.0, 0.0
+    ).astype(jnp.float32)
+    raw_all[here] = jnp.dot(
+        stacked, unmix, preferred_element_type=jnp.float32, precision=lax.Precision.HIGHEST
+    )
+    raw_copies = [
+        send(raw_all.at[here], raw_all.at[here], raw_send_sems.at[k], raw_recv_sems.at[k], plane_at(k))
+        for k in range(1, plane)
+    ]
+
+    scatter = jnp.concatenate(
+        [
+            one_hot(token_of(0, (2 * tok, STRETCH)) == iota((2 * tok, STRETCH), 1) + firsts[r])
+            for r in range(slots)
+        ],
+        axis=1,
+    )
+    row_scale = jnp.where(iota((WIDE, depth), 0) % 2 == 0, scale, 1.0)
+    row_copies = []
+    for h in range(heads):
+        parts = []
+        for r in range(slots):
+            mix = mixed[h, r]
+            out = dot(mix, kv_ref[r, h])
+            parts.append(jnp.concatenate([out[STRETCH:], out[:STRETCH] * scale], axis=1).astype(jnp.bfloat16))
+        rows = dot(scatter, jnp.concatenate(parts, axis=0))
+        rows_own[h] = rows[:tok]
+        rows_send[h] = rows[tok:].astype(jnp.bfloat16)
+        row_copies.append(send(rows_send.at[h], rows_recv.at[h], row_send_sems.at[h], row_recv_sems.at[h], peer))
+    for h in range(heads):
+        for r in range(slots):
+            dkv = dot(mixed[h, r], windows[h, r], ((0,), (0,))) * row_scale
+            dkv_ref[r, h] = dkv.astype(jnp.bfloat16)
+
+    for copy in raw_copies:
+        copy.wait_recv()
+    raw = raw_all[0]
+    for k in range(1, plane):
+        raw = raw + raw_all[k]
+    norm_all[mp] = jnp.broadcast_to(jnp.sum(raw * raw, keepdims=True), (8, 128))
+    norm_copies = [
+        send(norm_all.at[mp], norm_all.at[mp], norm_send_sems.at[k], norm_recv_sems.at[k], mp_at(k))
+        for k in range(1, mps)
+    ]
+    for h in range(heads):
+        row_copies[h].wait_recv()
+        rows = rows_own[h] + rows_recv[h].astype(jnp.float32)
+        cols = pl.ds(h * depth, depth)
+        att_ref[:, cols] = rows[:, :depth].astype(jnp.bfloat16)
+        dq_ref[:, cols] = rows[:, depth:].astype(jnp.bfloat16)
+    for copy in norm_copies:
+        copy.wait_recv()
+    squares = norm_all[0]
+    for k in range(1, mps):
+        squares = squares + norm_all[k]
+    clip = jnp.minimum(1.0, 1.0 / jnp.sqrt(squares[:, :1] + 1e-12))
+    dbias_ref[...] = (raw * clip)[: dbias_ref.shape[0], : dbias_ref.shape[1]]
+    for pair in in_copies:
+        for copy in pair:
+            copy.wait_send()
+    stat_copy.wait_send()
+    for copy in raw_copies + row_copies + norm_copies:
+        copy.wait_send()
+
+
+def pair_exchange(queries, d_out, neighbour_kv, target, bias):
+    _, tok, width = queries.shape
+    heads, rel = bias.shape
+    depth = width // heads
+    slots = neighbour_kv.shape[1]
+    plane, mps = 2 * lax.axis_size("grp"), lax.axis_size("mp")
+    kv = neighbour_kv[0].reshape(slots, NB_LEN, 2, heads, depth).transpose(0, 3, 1, 2, 4)
+    kv = kv.reshape(slots, heads, WIDE, depth)
+    turned = lax.pad(bias[:, ::-1], jnp.float32(0), [(0, 0, 0), (0, 2 * WIDE - 2 * rel + 1, 1)])
+    vmem = pl.BlockSpec(memory_space=pltpu.VMEM)
+    f32, bf16, dma = jnp.float32, jnp.bfloat16, pltpu.SemaphoreType.DMA
+    att, dq, dkv, dbias = pl.pallas_call(
+        pair_kernel,
+        out_shape=(
+            jax.ShapeDtypeStruct((tok, width), bf16),
+            jax.ShapeDtypeStruct((tok, width), bf16),
+            jax.ShapeDtypeStruct(kv.shape, bf16),
+            jax.ShapeDtypeStruct((heads, rel), f32),
+        ),
+        in_specs=[vmem, vmem, vmem, pl.BlockSpec(memory_space=pltpu.SMEM), vmem],
+        out_specs=(vmem,) * 4,
+        scratch_shapes=[
+            pltpu.VMEM((heads, tok, depth), bf16),
+            pltpu.VMEM((heads, tok, depth), bf16),
+            pltpu.VMEM((heads, slots, 2 * STRETCH, depth), bf16),
+            pltpu.VMEM((heads, slots, STRETCH, WIDE), f32),
+            pltpu.VMEM((heads, slots, STRETCH, WIDE), f32),
+            pltpu.VMEM((heads, slots, 2 * STRETCH, WIDE), bf16),
+            pltpu.VMEM((heads, tok, 2 * depth), f32),
+            pltpu.VMEM((heads, tok, 2 * depth), bf16),
+            pltpu.VMEM((heads, tok, 2 * depth), bf16),
+            pltpu.VMEM((STRETCH, 128), f32),
+            pltpu.VMEM((STRETCH, 128), f32),
+            pltpu.VMEM((plane, 8, WIDE), f32),
+            pltpu.VMEM((mps, 8, 128), f32),
+            dma((2 * heads,)),
+            dma((2 * heads,)),
+            dma((2,)),
+            dma((heads,)),
+            dma((heads,)),
+            dma((plane,)),
+            dma((plane,)),
+            dma((mps,)),
+            dma((mps,)),
+        ],
+        compiler_params=pltpu.CompilerParams(
+            collective_id=0, has_side_effects=True, vmem_limit_bytes=24 * 1024 * 1024
+        ),
+    )(queries[0], d_out[0], kv, target, turned)
+    dkv = dkv.reshape(slots, heads, NB_LEN, 2, depth).transpose(0, 2, 3, 1, 4)
+    dkv = dkv.reshape(slots, NB_LEN, 2, width)
+    return att[None], dq[None], dkv[None], dbias
+
+
+def local(queries, d_out, neighbour_kv, target, bias):
+    tok = queries.shape[1]
+    fits = (
+        lax.axis_size("seq") == 2
+        and neighbour_kv.shape[1] == 2 * (tok // STRETCH)
+        and tok == 128
+        and bias.shape == (4, 191)
+        and queries.shape[2] == 512
+    )
+    run = pair_exchange if fits else shard_exchange
+    return run(queries, d_out, neighbour_kv, target, bias)
+
+
 def solution(mesh):
     in_specs = (
         P("grp", "seq", "mp"),

time: 129 us -> 36 us (0.28)
  starting transfers between devices: 33 us -> 0 us
  blocking collectives: 27.3 us -> 0 us
  Pallas kernels: 0 us -> 26.2 us
  waiting for transfers between devices: 18.6 us -> 0 us
  other arithmetic: 14.2 us -> 0 us
  matrix products: 13.7 us -> 0 us
  local copies, waits for them, and re-layouts: 19 us -> 8.91 us
  between operations: 2.11 us -> 0.71 us
    all_to_all x8 -> x0, starting transfers between devices: 28.7 us -> none  [the longest x1 4.21 us: local(): lax.all_to_all(id_buffer, 'seq', split_axis=0, concat_axis=0, tiled=True)]
    psum x2 -> x0, blocking collectives: 27.3 us -> none  [the longest x1 14.2 us: local(): raw_sum = lax.psum(bias_part, ('grp', 'seq'))]
    pallas_call x0 -> x1, Pallas kernels: none -> 26.2 us  [pair_exchange(): pl.pallas_call(pair_kernel, out_shape=(jax.ShapeDtypeStruct((tok, width),...]
    all_to_all x8 -> x0, waiting for transfers between devices: 18.6 us -> none  [the longest x1 4.85 us: local(): lax.all_to_all(part_send, 'seq', split_axis=0, concat_axis=0, tiled=True)]
    dot_general x20 -> x0, matrix products: 13.7 us -> none  [the longest x14 11.1 us: select_rows(): jnp.dot(picker.astype(lookup.dtype), lookup, preferred_element_type=jnp.f...]
    reshape x19 -> x0, local copies, waits for them, and re-layouts: 6.07 us -> none  [the longest x1 1.49 us: local(): rows_recv.reshape(shard_count * capacity, -1)]
    ppermute x2 -> x0, starting transfers between devices: 4.34 us -> none  [passed_along(): return lax.ppermute(block, axis, route)]
    another operation x4 -> x0, other arithmetic: 3.25 us -> none  [the longest x1 3.21 us: local(): jnp.stack([grad_keys.reshape(slot_count, NB_LEN, width_dev), grad_values....]
  transfers between devices with their start and end apart: 10 -> 0, of which waited for: 5 -> 0; matrix products, arithmetic and copies ran while one was open for 23% -> 0% of each run, Pallas kernels for 0% -> 0%
where the time goes in v1:
time: 36 us; the launch traced here: 35.8 us
  Pallas kernels  26.2 us (73%)
  local copies, waits for them, and re-layouts  8.91 us (25%)
  between operations  0.71 us (2%)
    pallas_call x1, Pallas kernels, pair_exchange(): pl.pallas_call(pair_kernel, out_shape=(jax.ShapeDtypeStruct((tok, width),...  26.2 us
    unnamed x13, local copies, waits for them, and re-layouts  3.5 us
    another operation x2, local copies, waits for them, and re-layouts, pair_exchange(): neighbour_kv[0].reshape(slots, NB_LEN, 2, heads, depth)  2.62 us
    transpose x1, local copies, waits for them, and re-layouts, pair_exchange(): dkv = dkv.reshape(slots, heads, NB_LEN, 2, depth).transpose(0, 2, 3, 1, 4)  1.35 us
    another operation x1, local copies, waits for them, and re-layouts, pair_exchange(): return (att[None], dq[None], dkv[None], dbias)  1.22 us

profile of v1, /device:TPU:0, one launch (start us, length us, event | category | flops | bytes accessed | tf_op | source)
XLA Modules:
  0.0 35.8 jit_solution(7616553761102980389)
XLA Ops:
  0.6 0.0 copy-start.3
  0.6 0.7 %copy-done.3 = f32[4,191]{1,0:T(4,128)S(1)} copy-done((f32[4,191]{1,0:T(4,128)S(1)}, f32[4,191]{1,0:T(4,128)}, u32[]{:S(2)}) %copy-start.3) | copy-done | bytes 3080
  1.3 0.2 reverse
  1.5 0.1 slice
  1.6 0.2 pad.3.bias_ref
  1.8 1.7 %reshape_squeeze.3 = bf16[4,128,2,4,128]{4,3,2,1,0:T(4,128)(2,1)S(1)} reshape(bf16[1,4,128,2,512]{4,3,2,1,0:T(2,128)(2,1)} %param.7) | data formatting | bytes 2097152 | tf_op jit(solution)/shard_map/reshape;squeeze | solution.py:435
  3.5 0.0 copy-start
  3.5 0.0 copy-start.1
  3.6 0.9 %copy.9 = bf16[4,128,2,4,128]{4,2,1,3,0:T(2,128)(2,1)S(1)} copy(bf16[4,128,2,4,128]{4,3,2,1,0:T(4,128)(2,1)S(1)} %reshape_squeeze.3) | data formatting | bytes 2097152 | tf_op jit(solution)/shard_map/reshape;squeeze | solution.py:435
  4.4 0.0 copy-start.2
  4.5 0.0 copy-done
  4.5 0.0 copy-done.1
  4.5 0.6 %copy-done.2 = s32[1,4]{1,0:T(1,128)S(1)} copy-done((s32[1,4]{1,0:T(1,128)S(1)}, s32[1,4]{1,0:T(1,128)}, u32[]{:S(2)}) %copy-start.2) | copy-done | bytes 40
  5.1 26.2 %shard_map.84 = (bf16[128,512]{1,0:T(8,128)(2,1)S(1)}, bf16[128,512]{1,0:T(8,128)(2,1)S(1)}, bf16[4,4,256,128]{3,2,1,0:T(8,128)(2,1)S(1)}, f32[4,191]{1,0:T(4,128)S(1)}) custom-call(bf16[128,512]{1,0:T(8,128)(2,1)S(1)} %bitcast.13, bf16[128,512]{1,0:T(8,128)(2,1)S(1)} %bitcast.14, bf16[4,4,256,128]{3,2,1,0:T(8,128)(2,1)S(1)} %bitcast.11, ...), custom_call_target="tpu_custom_call" | custom-call | tf_op jit(solution)/shard_map/pallas_call | solution.py:440
  31.3 1.4 %copy.10 = bf16[4,128,2,4,128]{4,3,2,1,0:T(4,128)(2,1)S(1)} copy(bf16[4,128,2,4,128]{4,2,1,3,0:T(2,128)(2,1)S(1)} %bitcast.12) | data formatting | bytes 2097152 | tf_op jit(solution)/shard_map/transpose | solution.py:478
  32.7 1.2 %broadcast_in_dim_reshape.3 = bf16[1,4,128,2,512]{4,3,2,1,0:T(2,128)(2,1)} reshape(bf16[4,128,2,4,128]{4,3,2,1,0:T(4,128)(2,1)S(1)} %copy.10) | data formatting | bytes 2097152 | tf_op jit(solution)/shard_map/broadcast_in_dim;reshape | solution.py:480
  33.9 0.7 %copy.14 = bf16[1,128,512]{2,1,0:T(8,128)(2,1)} copy(bf16[1,128,512]{2,1,0:T(8,128)(2,1)S(1)} %bitcast.16) | data formatting | bytes 262144
  34.5 0.7 %copy.15 = bf16[1,128,512]{2,1,0:T(8,128)(2,1)} copy(bf16[1,128,512]{2,1,0:T(8,128)(2,1)S(1)} %bitcast.15) | data formatting | bytes 262144
  35.2 0.6 %copy.16 = f32[4,191]{1,0:T(4,128)} copy(f32[4,191]{1,0:T(4,128)S(1)} %get-tuple-element.19) | data formatting | bytes 6112
Async XLA Ops:
  0.6 0.7 %copy-start.3 = (f32[4,191]{1,0:T(4,128)S(1)}, f32[4,191]{1,0:T(4,128)}, u32[]{:S(2)}) copy-start(f32[4,191]{1,0:T(4,128)} %param.9) | copy-start | bytes 9172
  3.5 0.9 %copy-start = (bf16[1,128,512]{2,1,0:T(8,128)(2,1)S(1)}, bf16[1,128,512]{2,1,0:T(8,128)(2,1)}, u32[]{:S(2)}) copy-start(bf16[1,128,512]{2,1,0:T(8,128)(2,1)} %param.5) | copy-start | bytes 393220
  3.5 1.0 %copy-start.1 = (bf16[1,128,512]{2,1,0:T(8,128)(2,1)S(1)}, bf16[1,128,512]{2,1,0:T(8,128)(2,1)}, u32[]{:S(2)}) copy-start(bf16[1,128,512]{2,1,0:T(8,128)(2,1)} %param.6) | copy-start | bytes 393220
  4.4 0.7 %copy-start.2 = (s32[1,4]{1,0:T(1,128)S(1)}, s32[1,4]{1,0:T(1,128)}, u32[]{:S(2)}) copy-start(s32[1,4]{1,0:T(1,128)} %target_ref.1) | copy-start | bytes 52

commit v2 on v1

--- a/solution.py
+++ b/solution.py
@@ -224,16 +224,17 @@
 
 
 def pair_kernel(
-    q_ref, g_ref, kv_ref, target_ref, bias_ref,
+    q_hbm, g_hbm, kv_hbm, target_hbm, bias_ref,
     att_ref, dq_ref, dkv_ref, dbias_ref,
-    q_peer, g_peer, windows, weights, cotangents, mixed, rows_own, rows_send, rows_recv,
+    target_ref, q_ref, g_ref, kv_pairs, kv_ref, q_peer, g_peer, windows, weights, cotangents, mixed, rows_own, rows_send, rows_recv,
     stat_send, stat_recv, raw_all, norm_all,
-    in_send, in_recv, stat_sems, row_send_sems, row_recv_sems,
+    own_sems, kv_sems, in_send, in_recv, stat_send_sems, stat_recv_sems, row_send_sems, row_recv_sems,
     raw_send_sems, raw_recv_sems, norm_send_sems, norm_recv_sems,
 ):
     heads = bias_ref.shape[0]
     slots = kv_ref.shape[0]
     tok = q_ref.shape[0]
+    group = heads // 2
     depth = kv_ref.shape[-1]
     groups, mps = lax.axis_size("grp"), lax.axis_size("mp")
     plane = 2 * groups
@@ -249,6 +250,21 @@
     def mp_at(step):
         return {"mp": lax.rem(mp + step, mps)}
 
+    own_copies = [
+        pltpu.make_async_copy(target_hbm, target_ref, own_sems.at[0]),
+        pltpu.make_async_copy(q_hbm.at[0], q_ref, own_sems.at[1]),
+        pltpu.make_async_copy(g_hbm.at[0], g_ref, own_sems.at[2]),
+    ]
+    for copy in own_copies:
+        copy.start()
+    kv_copies = {}
+    for h in range(heads):
+        for r in range(slots):
+            kv_copies[h, r] = pltpu.make_async_copy(
+                kv_hbm.at[0, r, :, :, pl.ds(h * depth, depth)], kv_pairs.at[h, r], kv_sems.at[h, r]
+            )
+            kv_copies[h, r].start()
+
     barrier = pltpu.get_barrier_semaphore()
     for step in range(1, plane):
         pl.semaphore_signal(barrier, inc=1, device_id=plane_at(step), device_id_type=MESH)
@@ -268,10 +284,12 @@
     for h in range(heads):
         cols = pl.ds(h * depth, depth)
         in_copies.append((
-            send(q_ref.at[:, cols], q_peer.at[h], in_send.at[2 * h], in_recv.at[2 * h], peer),
-            send(g_ref.at[:, cols], g_peer.at[h], in_send.at[2 * h + 1], in_recv.at[2 * h + 1], peer),
+            send(q_hbm.at[0, :, cols], q_peer.at[h], in_send.at[2 * h], in_recv.at[2 * h], peer),
+            send(g_hbm.at[0, :, cols], g_peer.at[h], in_send.at[2 * h + 1], in_recv.at[2 * h + 1], peer),
         ))
 
+    for copy in own_copies:
+        copy.wait()
     entries = [target_ref[0, r] for r in range(slots)]
     firsts = [(STRETCH - 1) + STRETCH * (e // 2) for e in entries]
 
@@ -290,10 +308,23 @@
         axis=0,
     )
     odd = iota((STRETCH, WIDE), 1) % 2 == 1
+    rel = bias_ref.shape[1]
+    turn = jnp.where(
+        iota((rel, 2 * WIDE), 1) == 2 * (rel - 1) - 2 * iota((rel, 2 * WIDE), 0), 1.0, 0.0
+    ).astype(jnp.float32)
+    turned = jnp.dot(
+        bias_ref[...], turn, preferred_element_type=jnp.float32, precision=lax.Precision.HIGHEST
+    )
+    for h in range(heads):
+        for r in range(slots):
+            kv_copies[h, r].wait()
+            kv_ref[r, h] = kv_pairs[h, r].reshape(WIDE, depth)
     lane = iota((STRETCH, 128), 1)
-    table = jnp.zeros((STRETCH, 128), jnp.float32)
+    stat_copies = []
     for h in range(heads):
-        wide = jnp.broadcast_to(bias_ref[h : h + 1, :], (STRETCH, 2 * WIDE))
+        if h % group == 0:
+            table = jnp.zeros((STRETCH, 128), jnp.float32)
+        wide = jnp.broadcast_to(turned[h : h + 1, :], (STRETCH, 2 * WIDE))
         grid = pltpu.roll(wide, 2 * WIDE - 126, 1, stride=2, stride_axis=0)[:, :WIDE]
         grid = jnp.where(odd, -1e30, grid)
         cols = pl.ds(h * depth, depth)
@@ -320,25 +351,42 @@
             table = jnp.where(lane == base, peak, table)
             table = jnp.where(lane == base + 32, total, table)
             table = jnp.where(lane == base + 64, inner, table)
-    stat_send[...] = table
-    stat_copy = send(stat_send, stat_recv, stat_sems.at[0], stat_sems.at[1], peer)
-    stat_copy.wait_recv()
-    table = table + stat_recv[...]
+        if h % group == group - 1:
+            part = h // group
+            stat_send[part] = table
+            stat_copies.append(send(
+                stat_send.at[part], stat_recv.at[part],
+                stat_send_sems.at[part], stat_recv_sems.at[part], peer,
+            ))
 
     def partner(x):
         return jnp.where((lane // heads) % 2 == 0, pltpu.roll(x, 128 - heads, 1), pltpu.roll(x, heads, 1))
 
-    total = pltpu.roll(table, 96, 1)
-    inner = pltpu.roll(table, 64, 1)
-    other_peak = partner(table)
-    top = jnp.maximum(table, other_peak)
-    mine_f, other_f = jnp.exp(table - top), jnp.exp(other_peak - top)
-    denominator = mine_f * total + other_f * partner(total)
-    inner = (mine_f * inner + other_f * partner(inner)) / denominator
-    norm = mine_f / denominator
-
+    scatter = jnp.concatenate(
+        [
+            one_hot(token_of(0, (2 * tok, STRETCH)) == iota((2 * tok, STRETCH), 1) + firsts[r])
+            for r in range(slots)
+        ],
+        axis=1,
+    )
+    row8 = iota((8, 2 * WIDE), 0)
+    stacked = jnp.zeros((8, 2 * WIDE), jnp.float32)
+    row_copies = []
     for h in range(heads):
+        if h % group == 0:
+            part = h // group
+            stat_copies[part].wait_recv()
+            table = stat_send[part] + stat_recv[part]
+            total = pltpu.roll(table, 96, 1)
+            inner = pltpu.roll(table, 64, 1)
+            other_peak = partner(table)
+            top = jnp.maximum(table, other_peak)
+            mine_f, other_f = jnp.exp(table - top), jnp.exp(other_peak - top)
+            denominator = mine_f * total + other_f * partner(total)
+            inner = (mine_f * inner + other_f * partner(inner)) / denominator
+            norm = mine_f / denominator
         bias_sum = jnp.zeros((STRETCH, WIDE), jnp.float32)
+        parts = []
         for r in range(slots):
             at = lane == entries[r] * heads + h
             factor = jnp.sum(jnp.where(at, norm, 0.0), axis=1, keepdims=True)
@@ -346,55 +394,42 @@
             prob = weights[h, r] * factor
             grad = prob * (cotangents[h, r] - shift)
             bias_sum = bias_sum + grad
-            mixed[h, r, :STRETCH] = pltpu.roll(grad, WIDE - 1, 1).astype(jnp.bfloat16)
-            mixed[h, r, STRETCH:] = prob.astype(jnp.bfloat16)
-        folded = jnp.concatenate([bias_sum, jnp.zeros_like(bias_sum)], axis=1)
-        half = STRETCH // 2
-        while half >= 8:
-            folded = pltpu.roll(folded[:half], 2 * half, 1) + folded[half:]
-            half //= 2
-        row8 = iota((8, 2 * WIDE), 0)
-        for bit in (4, 2, 1):
-            folded = jnp.where((row8 // bit) % 2 == 0, pltpu.roll(folded, 2 * bit, 1), folded)
-        folded = jnp.sum(folded, axis=0, keepdims=True)
-        if h == 0:
-            stacked = jnp.zeros((8, 2 * WIDE), jnp.float32)
-        stacked = jnp.where(row8 == h, folded, stacked)
-    unmix = jnp.where(
-        iota((2 * WIDE, WIDE), 0) == 381 - 2 * iota((2 * WIDE, WIDE), 1), 1.0, 0.0
-    ).astype(jnp.float32)
-    raw_all[here] = jnp.dot(
-        stacked, unmix, preferred_element_type=jnp.float32, precision=lax.Precision.HIGHEST
-    )
-    raw_copies = [
-        send(raw_all.at[here], raw_all.at[here], raw_send_sems.at[k], raw_recv_sems.at[k], plane_at(k))
-        for k in range(1, plane)
-    ]
-
-    scatter = jnp.concatenate(
-        [
-            one_hot(token_of(0, (2 * tok, STRETCH)) == iota((2 * tok, STRETCH), 1) + firsts[r])
-            for r in range(slots)
-        ],
-        axis=1,
-    )
-    row_scale = jnp.where(iota((WIDE, depth), 0) % 2 == 0, scale, 1.0)
-    row_copies = []
-    for h in range(heads):
-        parts = []
-        for r in range(slots):
-            mix = mixed[h, r]
+            mix = jnp.concatenate([pltpu.roll(grad, WIDE - 1, 1), prob], axis=0).astype(jnp.bfloat16)
+            mixed[h, r] = mix
             out = dot(mix, kv_ref[r, h])
             parts.append(jnp.concatenate([out[STRETCH:], out[:STRETCH] * scale], axis=1).astype(jnp.bfloat16))
         rows = dot(scatter, jnp.concatenate(parts, axis=0))
         rows_own[h] = rows[:tok]
         rows_send[h] = rows[tok:].astype(jnp.bfloat16)
         row_copies.append(send(rows_send.at[h], rows_recv.at[h], row_send_sems.at[h], row_recv_sems.at[h], peer))
-    for h in range(heads):
-        for r in range(slots):
-            dkv = dot(mixed[h, r], windows[h, r], ((0,), (0,))) * row_scale
-            dkv_ref[r, h] = dkv.astype(jnp.bfloat16)
-
+        folded = jnp.concatenate([bias_sum, jnp.zeros_like(bias_sum)], axis=1)
+        half = STRETCH // 2
+        while half >= 8:
+            folded = pltpu.roll(folded[:half], 2 * half, 1) + folded[half:]
+            half //= 2
+        for bit in (4, 2, 1):
+            folded = jnp.where((row8 // bit) % 2 == 0, pltpu.roll(folded, 2 * bit, 1), folded)
+        stacked = jnp.where(row8 == h, jnp.sum(folded, axis=0, keepdims=True), stacked)
+    unmix = jnp.where(
+        iota((2 * WIDE, WIDE), 0) == 2 * rel - 1 - 2 * iota((2 * WIDE, WIDE), 1), 1.0, 0.0
+    ).astype(jnp.float32)
+    raw_all[here] = jnp.dot(
+        stacked, unmix, preferred_element_type=jnp.float32, precision=lax.Precision.HIGHEST
+    )
+    raw_copies = [
+        send(raw_all.at[here], raw_all.at[here], raw_send_sems.at[k], raw_recv_sems.at[k], plane_at(k))
+        for k in range(1, plane)
+    ]
+
+    row_scale = jnp.where(iota((WIDE, depth), 0) % 2 == 0, scale, 1.0)
+
+    def finish_kv(some_heads):
+        for h in some_heads:
+            for r in range(slots):
+                dkv = dot(mixed[h, r], windows[h, r], ((0,), (0,))) * row_scale
+                dkv_ref[r, h] = dkv.astype(jnp.bfloat16).reshape(NB_LEN, 2, depth)
+
+    finish_kv(range(group))
     for copy in raw_copies:
         copy.wait_recv()
     raw = raw_all[0]
@@ -405,6 +440,7 @@
         send(norm_all.at[mp], norm_all.at[mp], norm_send_sems.at[k], norm_recv_sems.at[k], mp_at(k))
         for k in range(1, mps)
     ]
+    finish_kv(range(group, heads))
     for h in range(heads):
         row_copies[h].wait_recv()
         rows = rows_own[h] + rows_recv[h].astype(jnp.float32)
@@ -421,9 +457,26 @@
     for pair in in_copies:
         for copy in pair:
             copy.wait_send()
-    stat_copy.wait_send()
-    for copy in raw_copies + row_copies + norm_copies:
+    for copy in stat_copies + raw_copies + row_copies + norm_copies:
         copy.wait_send()
+
+
+def write_kernel(att, dq, dkv, dbias, att_out, dq_out, dkv_out, dbias_out, sems, kv_sems):
+    copies = [
+        pltpu.make_async_copy(att, att_out.at[0], sems.at[0]),
+        pltpu.make_async_copy(dq, dq_out.at[0], sems.at[1]),
+    ]
+    slots, heads, _, _, depth = dkv.shape
+    for r in range(slots):
+        for h in range(heads):
+            copies.append(pltpu.make_async_copy(
+                dkv.at[r, h], dkv_out.at[0, r, :, :, pl.ds(h * depth, depth)], kv_sems.at[r, h]
+            ))
+    for copy in copies:
+        copy.start()
+    dbias_out[...] = dbias[...]
+    for copy in copies:
+        copy.wait()
 
 
 def pair_exchange(queries, d_out, neighbour_kv, target, bias):
@@ -432,22 +485,25 @@
     depth = width // heads
     slots = neighbour_kv.shape[1]
     plane, mps = 2 * lax.axis_size("grp"), lax.axis_size("mp")
-    kv = neighbour_kv[0].reshape(slots, NB_LEN, 2, heads, depth).transpose(0, 3, 1, 2, 4)
-    kv = kv.reshape(slots, heads, WIDE, depth)
-    turned = lax.pad(bias[:, ::-1], jnp.float32(0), [(0, 0, 0), (0, 2 * WIDE - 2 * rel + 1, 1)])
     vmem = pl.BlockSpec(memory_space=pltpu.VMEM)
+    hbm = pl.BlockSpec(memory_space=pltpu.HBM)
     f32, bf16, dma = jnp.float32, jnp.bfloat16, pltpu.SemaphoreType.DMA
-    att, dq, dkv, dbias = pl.pallas_call(
+    parts = pl.pallas_call(
         pair_kernel,
         out_shape=(
             jax.ShapeDtypeStruct((tok, width), bf16),
             jax.ShapeDtypeStruct((tok, width), bf16),
-            jax.ShapeDtypeStruct(kv.shape, bf16),
+            jax.ShapeDtypeStruct((slots, heads, NB_LEN, 2, depth), bf16),
             jax.ShapeDtypeStruct((heads, rel), f32),
         ),
-        in_specs=[vmem, vmem, vmem, pl.BlockSpec(memory_space=pltpu.SMEM), vmem],
+        in_specs=[hbm, hbm, hbm, hbm, vmem],
         out_specs=(vmem,) * 4,
         scratch_shapes=[
+            pltpu.SMEM(target.shape, jnp.int32),
+            pltpu.VMEM((tok, width), bf16),
+            pltpu.VMEM((tok, width), bf16),
+            pltpu.VMEM((heads, slots, NB_LEN, 2, depth), bf16),
+            pltpu.VMEM((slots, heads, WIDE, depth), bf16),
             pltpu.VMEM((heads, tok, depth), bf16),
             pltpu.VMEM((heads, tok, depth), bf16),
             pltpu.VMEM((heads, slots, 2 * STRETCH, depth), bf16),
@@ -457,12 +513,15 @@
             pltpu.VMEM((heads, tok, 2 * depth), f32),
             pltpu.VMEM((heads, tok, 2 * depth), bf16),
             pltpu.VMEM((heads, tok, 2 * depth), bf16),
-            pltpu.VMEM((STRETCH, 128), f32),
-            pltpu.VMEM((STRETCH, 128), f32),
+            pltpu.VMEM((2, STRETCH, 128), f32),
+            pltpu.VMEM((2, STRETCH, 128), f32),
             pltpu.VMEM((plane, 8, WIDE), f32),
             pltpu.VMEM((mps, 8, 128), f32),
+            dma((3,)),
+            dma((heads, slots)),
             dma((2 * heads,)),
             dma((2 * heads,)),
+            dma((2,)),
             dma((2,)),
             dma((heads,)),
             dma((heads,)),
@@ -474,10 +533,20 @@
         compiler_params=pltpu.CompilerParams(
             collective_id=0, has_side_effects=True, vmem_limit_bytes=24 * 1024 * 1024
         ),
-    )(queries[0], d_out[0], kv, target, turned)
-    dkv = dkv.reshape(slots, heads, NB_LEN, 2, depth).transpose(0, 2, 3, 1, 4)
-    dkv = dkv.reshape(slots, NB_LEN, 2, width)
-    return att[None], dq[None], dkv[None], dbias
+    )(queries, d_out, neighbour_kv, target, bias)
+    return pl.pallas_call(
+        write_kernel,
+        out_shape=(
+            jax.ShapeDtypeStruct(queries.shape, bf16),
+            jax.ShapeDtypeStruct(queries.shape, bf16),
+            jax.ShapeDtypeStruct(neighbour_kv.shape, bf16),
+            jax.ShapeDtypeStruct(bias.shape, f32),
+        ),
+        in_specs=[vmem] * 4,
+        out_specs=(hbm, hbm, hbm, vmem),
+        scratch_shapes=[dma((2,)), dma((slots, heads))],
+        compiler_params=pltpu.CompilerParams(vmem_limit_bytes=8 * 1024 * 1024),
+    )(*parts)
 
 
 def local(queries, d_out, neighbour_kv, target, bias):

time: 36 us -> 35.6 us (0.989)
  local copies, waits for them, and re-layouts: 8.91 us -> 4.37 us
  Pallas kernels: 26.2 us -> 30.3 us
    another operation x3 -> x0, local copies, waits for them, and re-layouts: 3.84 us -> none  [the longest x2 2.62 us: pair_exchange(): neighbour_kv[0].reshape(slots, NB_LEN, 2, heads, depth)]
    pallas_call x1, Pallas kernels: 26.2 us -> 28.5 us  [pair_exchange(): pl.pallas_call(pair_kernel, out_shape=(jax.ShapeDtypeStruct((tok, width),...]
    pallas_call x0 -> x1, Pallas kernels: none -> 1.8 us  [pair_exchange(): pl.pallas_call(write_kernel, out_shape=(jax.ShapeDtypeStruct(queries.shap...]
    transpose x1 -> x0, local copies, waits for them, and re-layouts: 1.35 us -> none  [pair_exchange(): dkv = dkv.reshape(slots, heads, NB_LEN, 2, depth).transpose(0, 2, 3, 1, 4)]
    unnamed x13 -> x10, local copies, waits for them, and re-layouts: 3.5 us -> 4.37 us
where the time goes in v2:
time: 35.6 us; the launch traced here: 35.4 us
  Pallas kernels  30.3 us (85%)
  local copies, waits for them, and re-layouts  4.37 us (12%)
  between operations  0.65 us (2%)
    pallas_call x1, Pallas kernels, pair_exchange(): pl.pallas_call(pair_kernel, out_shape=(jax.ShapeDtypeStruct((tok, width),...  28.5 us
    unnamed x10, local copies, waits for them, and re-layouts  4.37 us
    pallas_call x1, Pallas kernels, pair_exchange(): pl.pallas_call(write_kernel, out_shape=(jax.ShapeDtypeStruct(queries.shap...  1.8 us

profile of v2, /device:TPU:0, one launch (start us, length us, event | category | flops | bytes accessed | tf_op | source)
XLA Modules:
  0.0 35.4 jit_solution(14864044747605134585)
XLA Ops:
  0.6 0.0 copy-start
  0.6 1.2 %copy-done = bf16[1,4,128,2,512]{4,3,2,1,0:T(2,128)(2,1)S(1)} copy-done((bf16[1,4,128,2,512]{4,3,2,1,0:T(2,128)(2,1)S(1)}, bf16[1,4,128,2,512]{4,3,2,1,0:T(2,128)(2,1)}, u32[]{:S(2)}) %copy-start) | copy-done | bytes 1048600
  1.9 0.0 copy-start.1
  1.9 0.9 %copy-done.1 = bf16[1,128,512]{2,1,0:T(8,128)(2,1)S(1)} copy-done((bf16[1,128,512]{2,1,0:T(8,128)(2,1)S(1)}, bf16[1,128,512]{2,1,0:T(8,128)(2,1)}, u32[]{:S(2)}) %copy-start.1) | copy-done | bytes 131096
  2.8 0.0 copy-start.2
  2.8 0.9 %copy-done.2 = bf16[1,128,512]{2,1,0:T(8,128)(2,1)S(1)} copy-done((bf16[1,128,512]{2,1,0:T(8,128)(2,1)S(1)}, bf16[1,128,512]{2,1,0:T(8,128)(2,1)}, u32[]{:S(2)}) %copy-start.2) | copy-done | bytes 131096
  3.7 0.0 copy-start.3
  3.7 0.7 %copy-done.3 = f32[4,191]{1,0:T(4,128)S(1)} copy-done((f32[4,191]{1,0:T(4,128)S(1)}, f32[4,191]{1,0:T(4,128)}, u32[]{:S(2)}) %copy-start.3) | copy-done | bytes 3080
  4.4 0.0 copy-start.4
  4.4 0.7 %copy-done.4 = s32[1,4]{1,0:T(1,128)S(1)} copy-done((s32[1,4]{1,0:T(1,128)S(1)}, s32[1,4]{1,0:T(1,128)}, u32[]{:S(2)}) %copy-start.4) | copy-done | bytes 40
  5.0 28.5 %shard_map.84 = (bf16[128,512]{1,0:T(8,128)(2,1)S(1)}, bf16[128,512]{1,0:T(8,128)(2,1)S(1)}, bf16[4,4,128,2,128]{4,3,2,1,0:T(2,128)(2,1)S(1)}, f32[4,191]{1,0:T(4,128)S(1)}) custom-call(bf16[1,128,512]{2,1,0:T(8,128)(2,1)S(1)} %copy-done.1, bf16[1,128,512]{2,1,0:T(8,128)(2,1)S(1)} %copy-done.2, bf16[1,4,128,2,512]{4,3,2,1,0:T(2,128)(2,1)S(1)} %copy-done, ...), custom_call_target="tpu_custom_call" | custom-call | tf_op jit(solution)/shard_map/pallas_call | solution.py:491
  33.6 1.8 %shard_map.85 = (bf16[1,128,512]{2,1,0:T(8,128)(2,1)}, bf16[1,128,512]{2,1,0:T(8,128)(2,1)}, bf16[1,4,128,2,512]{4,3,2,1,0:T(2,128)(2,1)}, f32[4,191]{1,0:T(4,128)}) custom-call(bf16[128,512]{1,0:T(8,128)(2,1)S(1)} %get-tuple-element.8.att, bf16[128,512]{1,0:T(8,128)(2,1)S(1)} %get-tuple-element.9.dq, ...), custom_call_target="tpu_custom_call" | custom-call | tf_op jit(solution)/shard_map/pallas_call | solution.py:537
Async XLA Ops:
  0.6 1.2 %copy-start = (bf16[1,4,128,2,512]{4,3,2,1,0:T(2,128)(2,1)S(1)}, bf16[1,4,128,2,512]{4,3,2,1,0:T(2,128)(2,1)}, u32[]{:S(2)}) copy-start(bf16[1,4,128,2,512]{4,3,2,1,0:T(2,128)(2,1)} %kv_hbm.1) | copy-start | bytes 3145732
  1.9 0.9 %copy-start.1 = (bf16[1,128,512]{2,1,0:T(8,128)(2,1)S(1)}, bf16[1,128,512]{2,1,0:T(8,128)(2,1)}, u32[]{:S(2)}) copy-start(bf16[1,128,512]{2,1,0:T(8,128)(2,1)} %q_hbm.1) | copy-start | bytes 393220
  2.8 0.9 %copy-start.2 = (bf16[1,128,512]{2,1,0:T(8,128)(2,1)S(1)}, bf16[1,128,512]{2,1,0:T(8,128)(2,1)}, u32[]{:S(2)}) copy-start(bf16[1,128,512]{2,1,0:T(8,128)(2,1)} %g_hbm.1) | copy-start | bytes 393220
  3.7 0.7 %copy-start.3 = (f32[4,191]{1,0:T(4,128)S(1)}, f32[4,191]{1,0:T(4,128)}, u32[]{:S(2)}) copy-start(f32[4,191]{1,0:T(4,128)} %bias_ref.1) | copy-start | bytes 9172
  4.4 0.7 %copy-start.4 = (s32[1,4]{1,0:T(1,128)S(1)}, s32[1,4]{1,0:T(1,128)}, u32[]{:S(2)}) copy-start(s32[1,4]{1,0:T(1,128)} %target_hbm.1) | copy-start | bytes 52

commit v3 on v0

--- a/solution.py
+++ b/solution.py
@@ -1,6 +1,8 @@
 import jax
 import jax.numpy as jnp
 from jax import lax
+from jax.experimental import pallas as pl
+from jax.experimental.pallas import tpu as pltpu
 from jax.sharding import PartitionSpec as P
 
 STRETCH = 64
@@ -57,7 +59,7 @@
     return match_owner[:, None, :] & match_rank[None, :, :] & is_used[None, None, :]
 
 
-def local(queries, d_out, neighbour_kv, target, bias):
+def shard_exchange(queries, d_out, neighbour_kv, target, bias):
     tok_rows = queries.shape[1]
     width_dev = queries.shape[2]
     head_count = bias.shape[0]
@@ -208,6 +210,402 @@
     return (attended[None], d_query[None], d_kv[None], d_bias)
 
 
+WIDE = 2 * NB_LEN
+VMEM_USE = 60 * 1024 * 1024
+MESH = pl.DeviceIdType.MESH
+
+
+def dot(a, b, contract=((1,), (0,))):
+    return lax.dot_general(a, b, (contract, ((), ())), preferred_element_type=jnp.float32)
+
+
+def iota(shape, axis):
+    return lax.broadcasted_iota(jnp.int32, shape, axis)
+
+
+def pair_kernel(
+    q_hbm, g_hbm, kv_hbm, target_hbm, bias_ref,
+    att_hbm, dq_hbm, dkv_hbm, dbias_ref,
+    target_ref, q_ref, g_ref, kv_pairs, kv_ref, q_peer, g_peer,
+    windows, weights, cotangents, mixed, rows_own, rows_send, rows_recv,
+    gather_ref, scatter_ref, turned_ref, dkv_pairs, att_ref, dq_ref,
+    stat_send, stat_recv, raw_all, norm_all,
+    own_sems, kv_sems, in_send, in_recv, stat_send_sems, stat_recv_sems, row_send_sems, row_recv_sems,
+    raw_send_sems, raw_recv_sems, norm_send_sems, norm_recv_sems, out_sems, dkv_sems,
+):
+    heads, rel = bias_ref.shape
+    slots = kv_ref.shape[0]
+    tok = q_ref.shape[0]
+    depth = kv_ref.shape[-1]
+    group = heads // 2
+    groups, mps = lax.axis_size("grp"), lax.axis_size("mp")
+    plane = 2 * groups
+    scale = depth ** (-0.5)
+    grp, seq, mp = lax.axis_index("grp"), lax.axis_index("seq"), lax.axis_index("mp")
+    here = grp * 2 + seq
+    peer = {"seq": 1 - seq}
+
+    def plane_at(step):
+        there = lax.rem(here + step, plane)
+        return {"grp": there // 2, "seq": there % 2}
+
+    def mp_at(step):
+        return {"mp": lax.rem(mp + step, mps)}
+
+    def remote(src, dst, send_sem, recv_sem, device):
+        return pltpu.make_async_remote_copy(
+            src_ref=src, dst_ref=dst, send_sem=send_sem, recv_sem=recv_sem,
+            device_id=device, device_id_type=MESH,
+        )
+
+    def cols(h):
+        return pl.ds(pl.multiple_of(h * depth, depth), depth)
+
+    def q_copy(h):
+        return remote(q_hbm.at[0, :, cols(h)], q_peer.at[h], in_send.at[0, h], in_recv.at[0, h], peer)
+
+    def g_copy(h):
+        return remote(g_hbm.at[0, :, cols(h)], g_peer.at[h], in_send.at[1, h], in_recv.at[1, h], peer)
+
+    def kv_copy(h, r):
+        return pltpu.make_async_copy(kv_hbm.at[0, r, :, :, cols(h)], kv_pairs.at[h, r], kv_sems.at[h, r])
+
+    def stat_copy(part):
+        return remote(
+            stat_send.at[part], stat_recv.at[part], stat_send_sems.at[part], stat_recv_sems.at[part], peer
+        )
+
+    def row_copy(h):
+        return remote(rows_send.at[h], rows_recv.at[h], row_send_sems.at[h], row_recv_sems.at[h], peer)
+
+    def raw_copy(k):
+        return remote(raw_all.at[here], raw_all.at[here], raw_send_sems.at[k], raw_recv_sems.at[k], plane_at(k))
+
+    def norm_copy(k):
+        return remote(norm_all.at[mp], norm_all.at[mp], norm_send_sems.at[k], norm_recv_sems.at[k], mp_at(k))
+
+    def dkv_copy(h, r):
+        return pltpu.make_async_copy(dkv_pairs.at[h, r], dkv_hbm.at[0, r, :, :, cols(h)], dkv_sems.at[h, r])
+
+    def out_copies():
+        return (
+            pltpu.make_async_copy(att_ref, att_hbm.at[0], out_sems.at[0]),
+            pltpu.make_async_copy(dq_ref, dq_hbm.at[0], out_sems.at[1]),
+        )
+
+    def each(count, body):
+        def step(i, carry):
+            body(i)
+            return carry
+
+        lax.fori_loop(0, count, step, 0)
+
+    barrier = pltpu.get_barrier_semaphore()
+    for step in range(1, plane):
+        pl.semaphore_signal(barrier, inc=1, device_id=plane_at(step), device_id_type=MESH)
+    for step in range(1, mps):
+        pl.semaphore_signal(barrier, inc=1, device_id=mp_at(step), device_id_type=MESH)
+    own_copies = [
+        pltpu.make_async_copy(target_hbm, target_ref, own_sems.at[0]),
+        pltpu.make_async_copy(q_hbm.at[0], q_ref, own_sems.at[1]),
+        pltpu.make_async_copy(g_hbm.at[0], g_ref, own_sems.at[2]),
+    ]
+    for copy in own_copies:
+        copy.start()
+
+    def start_kv(h):
+        for r in range(slots):
+            kv_copy(h, r).start()
+
+    each(heads, start_kv)
+    pl.semaphore_wait(barrier, plane - 1 + mps - 1)
+
+    def start_rows(h):
+        q_copy(h).start()
+        g_copy(h).start()
+
+    each(heads, start_rows)
+
+    for copy in own_copies:
+        copy.wait()
+    entries = [target_ref[0, r] for r in range(slots)]
+
+    def token_of(axis, shape):
+        place = iota(shape, axis)
+        return jnp.where(place < tok, tok * seq + place, tok * (1 - seq) + place - tok)
+
+    def one_hot(flags):
+        return jnp.where(flags, 1.0, 0.0).astype(jnp.bfloat16)
+
+    for r in range(slots):
+        rows = pl.ds(r * STRETCH, STRETCH)
+        first = (STRETCH - 1) + STRETCH * (entries[r] // 2)
+        flat = (STRETCH, 2 * tok)
+        gather_ref[rows, :] = one_hot(token_of(1, flat) == iota(flat, 0) + first)
+    scatter_ref[...] = gather_ref[...].T
+    turn = jnp.where(
+        iota((rel, 2 * WIDE), 1) == 2 * (rel - 1) - 2 * iota((rel, 2 * WIDE), 0), 1.0, 0.0
+    ).astype(jnp.float32)
+    turned = jnp.dot(
+        bias_ref[...], turn, preferred_element_type=jnp.float32, precision=lax.Precision.HIGHEST
+    )
+    for h in range(heads):
+        turned_ref[h] = jnp.broadcast_to(turned[h : h + 1], (8, 2 * WIDE))
+    odd = iota((STRETCH, WIDE), 1) % 2 == 1
+    lane = iota((STRETCH, 128), 1)
+
+    def unpair(h):
+        for r in range(slots):
+            kv_copy(h, r).wait()
+            kv_ref[r, h] = kv_pairs[h, r].reshape(WIDE, depth)
+
+    each(heads, unpair)
+
+    def forward(h, table):
+        wide = jnp.broadcast_to(turned_ref[h][:1], (STRETCH, 2 * WIDE))
+        grid = pltpu.roll(wide, 2 * WIDE - 126, 1, stride=2, stride_axis=0)[:, :WIDE]
+        grid = jnp.where(odd, -1e30, grid)
+        mine = jnp.concatenate([q_ref[:, cols(h)], g_ref[:, cols(h)]], axis=1)
+        q_copy(h).wait_recv()
+        g_copy(h).wait_recv()
+        other = jnp.concatenate([q_peer[h], g_peer[h]], axis=1)
+        picked = dot(gather_ref[...], jnp.concatenate([mine, other], axis=0)).astype(jnp.bfloat16)
+        for r in range(slots):
+            rows = picked[r * STRETCH : (r + 1) * STRETCH]
+            both = jnp.concatenate([rows[:, :depth], rows[:, depth:]], axis=0)
+            windows[h, r] = both
+            prod = dot(both, kv_ref[r, h], ((1,), (1,)))
+            scores = prod[:STRETCH] * scale + grid
+            grad_prob = prod[STRETCH:]
+            peak = jnp.max(scores, axis=1, keepdims=True)
+            expd = jnp.exp(scores - peak)
+            total = jnp.sum(expd, axis=1, keepdims=True)
+            expd = pltpu.roll(expd, 1, 1)
+            inner = jnp.sum(expd * grad_prob, axis=1, keepdims=True)
+            weights[h, r] = expd
+            cotangents[h, r] = grad_prob
+            base = entries[r] * heads + h
+            table = jnp.where(lane == base, peak, table)
+            table = jnp.where(lane == base + 32, total, table)
+            table = jnp.where(lane == base + 64, inner, table)
+        return table
+
+    def forward_part(part):
+        table = jnp.zeros((STRETCH, 128), jnp.float32)
+        table = lax.fori_loop(part * group, part * group + group, forward, table)
+        stat_send[part] = table
+        stat_copy(part).start()
+
+    each(2, forward_part)
+
+    def partner(x):
+        return jnp.where((lane // heads) % 2 == 0, pltpu.roll(x, 128 - heads, 1), pltpu.roll(x, heads, 1))
+
+    row8 = iota((8, 2 * WIDE), 0)
+
+    def backward_part(part, stacked):
+        stat_copy(part).wait_recv()
+        table = stat_send[part] + stat_recv[part]
+        total = pltpu.roll(table, 96, 1)
+        inner = pltpu.roll(table, 64, 1)
+        other_peak = partner(table)
+        top = jnp.maximum(table, other_peak)
+        mine_f, other_f = jnp.exp(table - top), jnp.exp(other_peak - top)
+        denominator = mine_f * total + other_f * partner(total)
+        inner = (mine_f * inner + other_f * partner(inner)) / denominator
+        norm = mine_f / denominator
+
+        def backward(h, stacked):
+            bias_sum = jnp.zeros((STRETCH, WIDE), jnp.float32)
+            parts = []
+            for r in range(slots):
+                at = lane == entries[r] * heads + h
+                factor = jnp.sum(jnp.where(at, norm, 0.0), axis=1, keepdims=True)
+                shift = jnp.sum(jnp.where(at, inner, 0.0), axis=1, keepdims=True)
+                prob = weights[h, r] * factor
+                grad = prob * (cotangents[h, r] - shift)
+                bias_sum = bias_sum + grad
+                mix = jnp.concatenate([pltpu.roll(grad, WIDE - 1, 1), prob], axis=0).astype(jnp.bfloat16)
+                mixed[h, r] = mix
+                out = dot(mix, kv_ref[r, h])
+                parts.append(
+                    jnp.concatenate([out[STRETCH:], out[:STRETCH] * scale], axis=1).astype(jnp.bfloat16)
+                )
+            rows = dot(scatter_ref[...], jnp.concatenate(parts, axis=0))
+            rows_own[h] = rows[:tok]
+            rows_send[h] = rows[tok:].astype(jnp.bfloat16)
+            row_copy(h).start()
+            folded = jnp.concatenate([bias_sum, jnp.zeros_like(bias_sum)], axis=1)
+            half = STRETCH // 2
+            while half >= 8:
+                folded = pltpu.roll(folded[:half], 2 * half, 1) + folded[half:]
+                half //= 2
+            for bit in (4, 2, 1):
+                folded = jnp.where((row8 // bit) % 2 == 0, pltpu.roll(folded, 2 * bit, 1), folded)
+            return jnp.where(row8 == h, jnp.sum(folded, axis=0, keepdims=True), stacked)
+
+        return lax.fori_loop(part * group, part * group + group, backward, stacked)
+
+    stacked = lax.fori_loop(0, 2, backward_part, jnp.zeros((8, 2 * WIDE), jnp.float32))
+    unmix = jnp.where(
+        iota((2 * WIDE, WIDE), 0) == 2 * rel - 1 - 2 * iota((2 * WIDE, WIDE), 1), 1.0, 0.0
+    ).astype(jnp.float32)
+    raw_all[here] = jnp.dot(
+        stacked, unmix, preferred_element_type=jnp.float32, precision=lax.Precision.HIGHEST
+    )
+    for k in range(1, plane):
+        raw_copy(k).start()
+
+    row_scale = jnp.where(iota((WIDE, depth), 0) % 2 == 0, scale, 1.0)
+
+    def finish_kv(h):
+        for r in range(slots):
+            dkv = dot(mixed[h, r], windows[h, r], ((0,), (0,))) * row_scale
+            dkv_pairs[h, r] = dkv.astype(jnp.bfloat16).reshape(NB_LEN, 2, depth)
+            dkv_copy(h, r).start()
+
+    each(heads, finish_kv)
+    for k in range(1, plane):
+        raw_copy(k).wait_recv()
+    raw = raw_all[0]
+    for k in range(1, plane):
+        raw = raw + raw_all[k]
+    norm_all[mp] = jnp.broadcast_to(jnp.sum(raw * raw, keepdims=True), (8, 128))
+    for k in range(1, mps):
+        norm_copy(k).start()
+
+    def finish_rows(h):
+        row_copy(h).wait_recv()
+        rows = rows_own[h] + rows_recv[h].astype(jnp.float32)
+        att_ref[:, cols(h)] = rows[:, :depth].astype(jnp.bfloat16)
+        dq_ref[:, cols(h)] = rows[:, depth:].astype(jnp.bfloat16)
+
+    each(heads, finish_rows)
+    for copy in out_copies():
+        copy.start()
+    for k in range(1, mps):
+        norm_copy(k).wait_recv()
+    squares = norm_all[0]
+    for k in range(1, mps):
+        squares = squares + norm_all[k]
+    clip = jnp.minimum(1.0, 1.0 / jnp.sqrt(squares[:, :1] + 1e-12))
+    dbias_ref[...] = (raw * clip)[:heads, :rel]
+
+    def drain(h):
+        q_copy(h).wait_send()
+        g_copy(h).wait_send()
+        row_copy(h).wait_send()
+        for r in range(slots):
+            dkv_copy(h, r).wait()
+
+    each(heads, drain)
+    for part in range(2):
+        stat_copy(part).wait_send()
+    for k in range(1, plane):
+        raw_copy(k).wait_send()
+    for k in range(1, mps):
+        norm_copy(k).wait_send()
+    for copy in out_copies():
+        copy.wait()
+
+
+def write_kernel(att, dq, dkv, dbias, att_out, dq_out, dkv_out, dbias_out, sems):
+    slots = dkv.shape[1]
+    copies = [
+        pltpu.make_async_copy(att, att_out, sems.at[slots]),
+        pltpu.make_async_copy(dq, dq_out, sems.at[slots + 1]),
+        pltpu.make_async_copy(dbias, dbias_out, sems.at[slots + 2]),
+    ]
+    for r in range(slots):
+        copies.append(pltpu.make_async_copy(dkv.at[0, r], dkv_out.at[0, r], sems.at[r]))
+    for copy in copies:
+        copy.start()
+    for copy in copies:
+        copy.wait()
+
+
+def pair_exchange(queries, d_out, neighbour_kv, target, bias):
+    _, tok, width = queries.shape
+    heads = bias.shape[0]
+    depth = width // heads
+    slots = neighbour_kv.shape[1]
+    plane, mps = 2 * lax.axis_size("grp"), lax.axis_size("mp")
+    vmem = pl.BlockSpec(memory_space=pltpu.VMEM)
+    hbm = pl.BlockSpec(memory_space=pltpu.HBM)
+    f32, bf16, dma = jnp.float32, jnp.bfloat16, pltpu.SemaphoreType.DMA
+    results = tuple(jax.ShapeDtypeStruct(x.shape, x.dtype) for x in (queries, d_out, neighbour_kv, bias))
+    parts = pl.pallas_call(
+        pair_kernel,
+        out_shape=results,
+        in_specs=[hbm, hbm, hbm, hbm, vmem],
+        out_specs=(hbm, hbm, hbm, vmem),
+        scratch_shapes=[
+            pltpu.SMEM(target.shape, jnp.int32),
+            pltpu.VMEM((tok, width), bf16),
+            pltpu.VMEM((tok, width), bf16),
+            pltpu.VMEM((heads, slots, NB_LEN, 2, depth), bf16),
+            pltpu.VMEM((slots, heads, WIDE, depth), bf16),
+            pltpu.VMEM((heads, tok, depth), bf16),
+            pltpu.VMEM((heads, tok, depth), bf16),
+            pltpu.VMEM((heads, slots, 2 * STRETCH, depth), bf16),
+            pltpu.VMEM((heads, slots, STRETCH, WIDE), f32),
+            pltpu.VMEM((heads, slots, STRETCH, WIDE), f32),
+            pltpu.VMEM((heads, slots, 2 * STRETCH, WIDE), bf16),
+            pltpu.VMEM((heads, tok, 2 * depth), f32),
+            pltpu.VMEM((heads, tok, 2 * depth), bf16),
+            pltpu.VMEM((heads, tok, 2 * depth), bf16),
+            pltpu.VMEM((slots * STRETCH, 2 * tok), bf16),
+            pltpu.VMEM((2 * tok, slots * STRETCH), bf16),
+            pltpu.VMEM((heads, 8, 2 * WIDE), f32),
+            pltpu.VMEM((heads, slots, NB_LEN, 2, depth), bf16),
+            pltpu.VMEM((tok, width), bf16),
+            pltpu.VMEM((tok, width), bf16),
+            pltpu.VMEM((2, STRETCH, 128), f32),
+            pltpu.VMEM((2, STRETCH, 128), f32),
+            pltpu.VMEM((plane, 8, WIDE), f32),
+            pltpu.VMEM((mps, 8, 128), f32),
+            dma((3,)),
+            dma((heads, slots)),
+            dma((2, heads)),
+            dma((2, heads)),
+            dma((2,)),
+            dma((2,)),
+            dma((heads,)),
+            dma((heads,)),
+            dma((plane,)),
+            dma((plane,)),
+            dma((mps,)),
+            dma((mps,)),
+            dma((2,)),
+            dma((heads, slots)),
+        ],
+        compiler_params=pltpu.CompilerParams(
+            collective_id=0, has_side_effects=True, vmem_limit_bytes=VMEM_USE
+        ),
+    )(queries, d_out, neighbour_kv, target, bias)
+    return pl.pallas_call(
+        write_kernel,
+        out_shape=results,
+        in_specs=[hbm] * 4,
+        out_specs=(hbm,) * 4,
+        scratch_shapes=[dma((slots + 3,))],
+        compiler_params=pltpu.CompilerParams(vmem_limit_bytes=VMEM_USE),
+    )(*parts)
+
+
+def local(queries, d_out, neighbour_kv, target, bias):
+    tok = queries.shape[1]
+    fits = (
+        lax.axis_size("seq") == 2
+        and neighbour_kv.shape[1] == 2 * (tok // STRETCH)
+        and tok == 128
+        and bias.shape == (4, 191)
+        and queries.shape[2] == 512
+    )
+    run = pair_exchange if fits else shard_exchange
+    return run(queries, d_out, neighbour_kv, target, bias)
+
+
 def solution(mesh):
     in_specs = (
         P("grp", "seq", "mp"),

time: 129 us -> 71 us (0.55)
  Pallas kernels: 0 us -> 70.2 us
  starting transfers between devices: 33 us -> 0 us
  blocking collectives: 27.3 us -> 0 us
  local copies, waits for them, and re-layouts: 19 us -> 0 us
  waiting for transfers between devices: 18.6 us -> 0 us
  other arithmetic: 14.2 us -> 0 us
  matrix products: 13.7 us -> 0 us
  between operations: 2.11 us -> 0.64 us
    pallas_call x0 -> x2, Pallas kernels: none -> 70.2 us  [the longest x1 41 us: pair_exchange(): pl.pallas_call(write_kernel, out_shape=results, in_specs=[hbm] * 4, out_s...]
    all_to_all x8 -> x0, starting transfers between devices: 28.7 us -> none  [the longest x1 4.21 us: local(): lax.all_to_all(id_buffer, 'seq', split_axis=0, concat_axis=0, tiled=True)]
    psum x2 -> x0, blocking collectives: 27.3 us -> none  [the longest x1 14.2 us: local(): raw_sum = lax.psum(bias_part, ('grp', 'seq'))]
    all_to_all x8 -> x0, waiting for transfers between devices: 18.6 us -> none  [the longest x1 4.85 us: local(): lax.all_to_all(part_send, 'seq', split_axis=0, concat_axis=0, tiled=True)]
    dot_general x20 -> x0, matrix products: 13.7 us -> none  [the longest x14 11.1 us: select_rows(): jnp.dot(picker.astype(lookup.dtype), lookup, preferred_element_type=jnp.f...]
    reshape x19 -> x0, local copies, waits for them, and re-layouts: 6.07 us -> none  [the longest x1 1.49 us: local(): rows_recv.reshape(shard_count * capacity, -1)]
    ppermute x2 -> x0, starting transfers between devices: 4.34 us -> none  [passed_along(): return lax.ppermute(block, axis, route)]
    unnamed x41 -> x0, local copies, waits for them, and re-layouts: 3.97 us -> none
  transfers between devices with their start and end apart: 10 -> 0, of which waited for: 5 -> 0; matrix products, arithmetic and copies ran while one was open for 23% -> 0% of each run, Pallas kernels for 0% -> 0%
where the time goes in v3:
time: 71 us; the launch traced here: 70.9 us
  Pallas kernels  70.2 us (99%)
    pallas_call x1, Pallas kernels, pair_exchange(): pl.pallas_call(write_kernel, out_shape=results, in_specs=[hbm] * 4, out_s...  41 us
    pallas_call x1, Pallas kernels, pair_exchange(): pl.pallas_call(pair_kernel, out_shape=results, in_specs=[hbm, hbm, hbm, h...  29.2 us

profile of v3, /device:TPU:0, one launch (start us, length us, event | category | flops | bytes accessed | tf_op | source)
XLA Modules:
  0.0 70.9 jit_solution(7689783695367420482)
XLA Ops:
  0.6 29.2 %shard_map.84 = (bf16[1,128,512]{2,1,0:T(8,128)(2,1)}, bf16[1,128,512]{2,1,0:T(8,128)(2,1)}, bf16[1,4,128,2,512]{4,3,2,1,0:T(2,128)(2,1)}, f32[4,191]{1,0:T(4,128)}) custom-call(bf16[1,128,512]{2,1,0:T(8,128)(2,1)} %q_hbm.1, bf16[1,128,512]{2,1,0:T(8,128)(2,1)} %g_hbm.1, bf16[1,4,128,2,512]{4,3,2,1,0:T(2,128)(2,1)} %kv_hbm.1, s32[1,4]{1,0:T(1,128)} %target_hbm.1, ...), custom_call_target="tpu_custom_call" | custom-call | tf_op jit(solution)/shard_map/pallas_call | solution.py:537
  29.9 41.0 %shard_map.85 = (bf16[1,128,512]{2,1,0:T(8,128)(2,1)}, bf16[1,128,512]{2,1,0:T(8,128)(2,1)}, bf16[1,4,128,2,512]{4,3,2,1,0:T(2,128)(2,1)}, f32[4,191]{1,0:T(4,128)}) custom-call(bf16[1,128,512]{2,1,0:T(8,128)(2,1)} %get-tuple-element.8.att, bf16[1,128,512]{2,1,0:T(8,128)(2,1)} %get-tuple-element.9.dq, bf16[1,4,128,2,512]{4,3,2,1,0:T(2,128)(2,1)} %get-tuple-element.10.dkv, ...), custom_call_target="tpu_custom_call" | custom-call | tf_op jit(solution)/shard_map/pallas_call | solution.py:586

commit v4 on v3

--- a/solution.py
+++ b/solution.py
@@ -237,7 +237,9 @@
     slots = kv_ref.shape[0]
     tok = q_ref.shape[0]
     depth = kv_ref.shape[-1]
-    group = heads // 2
+    lead = (STRETCH - 1) // 16 * 16
+    late = pl.ds(lead, tok - lead)
+    early = pl.ds(0, lead)
     groups, mps = lax.axis_size("grp"), lax.axis_size("mp")
     plane = 2 * groups
     scale = depth ** (-0.5)
@@ -261,11 +263,21 @@
     def cols(h):
         return pl.ds(pl.multiple_of(h * depth, depth), depth)
 
-    def q_copy(h):
-        return remote(q_hbm.at[0, :, cols(h)], q_peer.at[h], in_send.at[0, h], in_recv.at[0, h], peer)
-
-    def g_copy(h):
-        return remote(g_hbm.at[0, :, cols(h)], g_peer.at[h], in_send.at[1, h], in_recv.at[1, h], peer)
+    def q_copy(h, rows, lane):
+        return remote(
+            q_hbm.at[0, rows, cols(h)], q_peer.at[h, rows], in_send.at[lane, h], in_recv.at[lane, h], peer
+        )
+
+    def g_copy(h, rows, lane):
+        return remote(
+            g_hbm.at[0, rows, cols(h)], g_peer.at[h, rows], in_send.at[lane, h], in_recv.at[lane, h], peer
+        )
+
+    def in_late(h):
+        return q_copy(h, late, 0), g_copy(h, late, 1)
+
+    def in_early(h):
+        return q_copy(h, early, 2), g_copy(h, early, 3)
 
     def kv_copy(h, r):
         return pltpu.make_async_copy(kv_hbm.at[0, r, :, :, cols(h)], kv_pairs.at[h, r], kv_sems.at[h, r])
@@ -275,8 +287,17 @@
             stat_send.at[part], stat_recv.at[part], stat_send_sems.at[part], stat_recv_sems.at[part], peer
         )
 
-    def row_copy(h):
-        return remote(rows_send.at[h], rows_recv.at[h], row_send_sems.at[h], row_recv_sems.at[h], peer)
+    def row_copy(h, rows, lane):
+        return remote(
+            rows_send.at[h, rows], rows_recv.at[h, rows],
+            row_send_sems.at[lane, h], row_recv_sems.at[lane, h], peer,
+        )
+
+    def row_late(h):
+        return row_copy(h, late, 0)
+
+    def row_early(h):
+        return row_copy(h, early, 1)
 
     def raw_copy(k):
         return remote(raw_all.at[here], raw_all.at[here], raw_send_sems.at[k], raw_recv_sems.at[k], plane_at(k))
@@ -321,10 +342,24 @@
     pl.semaphore_wait(barrier, plane - 1 + mps - 1)
 
     def start_rows(h):
-        q_copy(h).start()
-        g_copy(h).start()
+        for copy in in_late(h):
+            copy.start()
+
+        @pl.when(seq == 1)
+        def _():
+            for copy in in_early(h):
+                copy.start()
 
     each(heads, start_rows)
+
+    @pl.when(seq == 1)
+    def _():
+        q_peer[:, early] = jnp.zeros((heads, lead, depth), jnp.bfloat16)
+        g_peer[:, early] = jnp.zeros((heads, lead, depth), jnp.bfloat16)
+
+    @pl.when(seq == 0)
+    def _():
+        rows_recv[:, early] = jnp.zeros((heads, lead, 2 * depth), jnp.bfloat16)
 
     for copy in own_copies:
         copy.wait()
@@ -361,13 +396,20 @@
 
     each(heads, unpair)
 
-    def forward(h, table):
+    def forward(h):
+        table = jnp.zeros((STRETCH, 128), jnp.float32)
         wide = jnp.broadcast_to(turned_ref[h][:1], (STRETCH, 2 * WIDE))
         grid = pltpu.roll(wide, 2 * WIDE - 126, 1, stride=2, stride_axis=0)[:, :WIDE]
         grid = jnp.where(odd, -1e30, grid)
         mine = jnp.concatenate([q_ref[:, cols(h)], g_ref[:, cols(h)]], axis=1)
-        q_copy(h).wait_recv()
-        g_copy(h).wait_recv()
+        for copy in in_late(h):
+            copy.wait_recv()
+
+        @pl.when(seq == 0)
+        def _():
+            for copy in in_early(h):
+                copy.wait_recv()
+
         other = jnp.concatenate([q_peer[h], g_peer[h]], axis=1)
         picked = dot(gather_ref[...], jnp.concatenate([mine, other], axis=0)).astype(jnp.bfloat16)
         for r in range(slots):
@@ -384,69 +426,77 @@
             inner = jnp.sum(expd * grad_prob, axis=1, keepdims=True)
             weights[h, r] = expd
             cotangents[h, r] = grad_prob
-            base = entries[r] * heads + h
+            base = entries[r]
             table = jnp.where(lane == base, peak, table)
-            table = jnp.where(lane == base + 32, total, table)
-            table = jnp.where(lane == base + 64, inner, table)
-        return table
-
-    def forward_part(part):
-        table = jnp.zeros((STRETCH, 128), jnp.float32)
-        table = lax.fori_loop(part * group, part * group + group, forward, table)
-        stat_send[part] = table
-        stat_copy(part).start()
-
-    each(2, forward_part)
+            table = jnp.where(lane == base + 8, total, table)
+            table = jnp.where(lane == base + 16, inner, table)
+        quarter = STRETCH // 4
+        packed = table[:quarter]
+        for k in range(1, 4):
+            packed = packed + pltpu.roll(table[k * quarter : (k + 1) * quarter], 32 * k, 1)
+        stat_send[h] = packed
+        stat_copy(h).start()
 
     def partner(x):
-        return jnp.where((lane // heads) % 2 == 0, pltpu.roll(x, 128 - heads, 1), pltpu.roll(x, heads, 1))
+        return jnp.where(lane % 2 == 0, pltpu.roll(x, 127, 1), pltpu.roll(x, 1, 1))
 
     row8 = iota((8, 2 * WIDE), 0)
 
-    def backward_part(part, stacked):
-        stat_copy(part).wait_recv()
-        table = stat_send[part] + stat_recv[part]
-        total = pltpu.roll(table, 96, 1)
-        inner = pltpu.roll(table, 64, 1)
+    def backward(h, stacked):
+        stat_copy(h).wait_recv()
+        packed = stat_send[h] + stat_recv[h]
+        table = jnp.concatenate(
+            [packed] + [pltpu.roll(packed, 128 - 32 * k, 1) for k in range(1, 4)], axis=0
+        )
+        table = jnp.where(lane < 32, table, 0.0)
+        total = pltpu.roll(table, 120, 1)
+        inner = pltpu.roll(table, 112, 1)
         other_peak = partner(table)
         top = jnp.maximum(table, other_peak)
         mine_f, other_f = jnp.exp(table - top), jnp.exp(other_peak - top)
         denominator = mine_f * total + other_f * partner(total)
         inner = (mine_f * inner + other_f * partner(inner)) / denominator
         norm = mine_f / denominator
-
-        def backward(h, stacked):
-            bias_sum = jnp.zeros((STRETCH, WIDE), jnp.float32)
-            parts = []
-            for r in range(slots):
-                at = lane == entries[r] * heads + h
-                factor = jnp.sum(jnp.where(at, norm, 0.0), axis=1, keepdims=True)
-                shift = jnp.sum(jnp.where(at, inner, 0.0), axis=1, keepdims=True)
-                prob = weights[h, r] * factor
-                grad = prob * (cotangents[h, r] - shift)
-                bias_sum = bias_sum + grad
-                mix = jnp.concatenate([pltpu.roll(grad, WIDE - 1, 1), prob], axis=0).astype(jnp.bfloat16)
-                mixed[h, r] = mix
-                out = dot(mix, kv_ref[r, h])
-                parts.append(
-                    jnp.concatenate([out[STRETCH:], out[:STRETCH] * scale], axis=1).astype(jnp.bfloat16)
-                )
-            rows = dot(scatter_ref[...], jnp.concatenate(parts, axis=0))
-            rows_own[h] = rows[:tok]
-            rows_send[h] = rows[tok:].astype(jnp.bfloat16)
-            row_copy(h).start()
-            folded = jnp.concatenate([bias_sum, jnp.zeros_like(bias_sum)], axis=1)
-            half = STRETCH // 2
-            while half >= 8:
-                folded = pltpu.roll(folded[:half], 2 * half, 1) + folded[half:]
-                half //= 2
-            for bit in (4, 2, 1):
-                folded = jnp.where((row8 // bit) % 2 == 0, pltpu.roll(folded, 2 * bit, 1), folded)
-            return jnp.where(row8 == h, jnp.sum(folded, axis=0, keepdims=True), stacked)
-
-        return lax.fori_loop(part * group, part * group + group, backward, stacked)
-
-    stacked = lax.fori_loop(0, 2, backward_part, jnp.zeros((8, 2 * WIDE), jnp.float32))
+        bias_sum = jnp.zeros((STRETCH, WIDE), jnp.float32)
+        parts = []
+        for r in range(slots):
+            at = lane == entries[r]
+            factor = jnp.sum(jnp.where(at, norm, 0.0), axis=1, keepdims=True)
+            shift = jnp.sum(jnp.where(at, inner, 0.0), axis=1, keepdims=True)
+            prob = weights[h, r] * factor
+            grad = prob * (cotangents[h, r] - shift)
+            bias_sum = bias_sum + grad
+            mix = jnp.concatenate([pltpu.roll(grad, WIDE - 1, 1), prob], axis=0).astype(jnp.bfloat16)
+            mixed[h, r] = mix
+            out = dot(mix, kv_ref[r, h])
+            parts.append(
+                jnp.concatenate([out[STRETCH:], out[:STRETCH] * scale], axis=1).astype(jnp.bfloat16)
+            )
+        rows = dot(scatter_ref[...], jnp.concatenate(parts, axis=0))
+        rows_own[h] = rows[:tok]
+        rows_send[h] = rows[tok:].astype(jnp.bfloat16)
+        row_late(h).start()
+
+        @pl.when(seq == 0)
+        def _():
+            row_early(h).start()
+
+        folded = jnp.concatenate([bias_sum, jnp.zeros_like(bias_sum)], axis=1)
+        half = STRETCH // 2
+        while half >= 8:
+            folded = pltpu.roll(folded[:half], 2 * half, 1) + folded[half:]
+            half //= 2
+        for bit in (4, 2, 1):
+            folded = jnp.where((row8 // bit) % 2 == 0, pltpu.roll(folded, 2 * bit, 1), folded)
+        return jnp.where(row8 == h, jnp.sum(folded, axis=0, keepdims=True), stacked)
+
+    def both(h, stacked):
+        forward(h + 1)
+        return backward(h, stacked)
+
+    forward(0)
+    stacked = lax.fori_loop(0, heads - 1, both, jnp.zeros((8, 2 * WIDE), jnp.float32))
+    stacked = backward(heads - 1, stacked)
     unmix = jnp.where(
         iota((2 * WIDE, WIDE), 0) == 2 * rel - 1 - 2 * iota((2 * WIDE, WIDE), 1), 1.0, 0.0
     ).astype(jnp.float32)
@@ -464,7 +514,7 @@
             dkv_pairs[h, r] = dkv.astype(jnp.bfloat16).reshape(NB_LEN, 2, depth)
             dkv_copy(h, r).start()
 
-    each(heads, finish_kv)
+    each(heads // 2, finish_kv)
     for k in range(1, plane):
         raw_copy(k).wait_recv()
     raw = raw_all[0]
@@ -474,8 +524,15 @@
     for k in range(1, mps):
         norm_copy(k).start()
 
+    each(heads - heads // 2, lambda h: finish_kv(h + heads // 2))
+
     def finish_rows(h):
-        row_copy(h).wait_recv()
+        row_late(h).wait_recv()
+
+        @pl.when(seq == 1)
+        def _():
+            row_early(h).wait_recv()
+
         rows = rows_own[h] + rows_recv[h].astype(jnp.float32)
         att_ref[:, cols(h)] = rows[:, :depth].astype(jnp.bfloat16)
         dq_ref[:, cols(h)] = rows[:, depth:].astype(jnp.bfloat16)
@@ -492,15 +549,24 @@
     dbias_ref[...] = (raw * clip)[:heads, :rel]
 
     def drain(h):
-        q_copy(h).wait_send()
-        g_copy(h).wait_send()
-        row_copy(h).wait_send()
+        for copy in in_late(h):
+            copy.wait_send()
+        row_late(h).wait_send()
+        stat_copy(h).wait_send()
+
+        @pl.when(seq == 1)
+        def _():
+            for copy in in_early(h):
+                copy.wait_send()
+
+        @pl.when(seq == 0)
+        def _():
+            row_early(h).wait_send()
+
         for r in range(slots):
             dkv_copy(h, r).wait()
 
     each(heads, drain)
-    for part in range(2):
-        stat_copy(part).wait_send()
     for k in range(1, plane):
         raw_copy(k).wait_send()
     for k in range(1, mps):
@@ -509,18 +575,21 @@
         copy.wait()
 
 
-def write_kernel(att, dq, dkv, dbias, att_out, dq_out, dkv_out, dbias_out, sems):
+def write_kernel(
+    att, dq, dkv, dbias, att_out, dq_out, dkv_out, dbias_out,
+    att_held, dq_held, dkv_held, dbias_held, load_sems, store_sems,
+):
     slots = dkv.shape[1]
-    copies = [
-        pltpu.make_async_copy(att, att_out, sems.at[slots]),
-        pltpu.make_async_copy(dq, dq_out, sems.at[slots + 1]),
-        pltpu.make_async_copy(dbias, dbias_out, sems.at[slots + 2]),
-    ]
-    for r in range(slots):
-        copies.append(pltpu.make_async_copy(dkv.at[0, r], dkv_out.at[0, r], sems.at[r]))
-    for copy in copies:
+    routes = [(dkv.at[0, r], dkv_held.at[r], dkv_out.at[0, r]) for r in range(slots)]
+    routes += [(att, att_held, att_out), (dq, dq_held, dq_out), (dbias, dbias_held, dbias_out)]
+    loads = [pltpu.make_async_copy(a, b, load_sems.at[k]) for k, (a, b, _) in enumerate(routes)]
+    stores = [pltpu.make_async_copy(b, c, store_sems.at[k]) for k, (_, b, c) in enumerate(routes)]
+    for copy in loads:
         copy.start()
-    for copy in copies:
+    for load, store in zip(loads, stores):
+        load.wait()
+        store.start()
+    for copy in stores:
         copy.wait()
 
 
@@ -560,18 +629,18 @@
             pltpu.VMEM((heads, slots, NB_LEN, 2, depth), bf16),
             pltpu.VMEM((tok, width), bf16),
             pltpu.VMEM((tok, width), bf16),
-            pltpu.VMEM((2, STRETCH, 128), f32),
-            pltpu.VMEM((2, STRETCH, 128), f32),
+            pltpu.VMEM((heads, STRETCH // 4, 128), f32),
+            pltpu.VMEM((heads, STRETCH // 4, 128), f32),
             pltpu.VMEM((plane, 8, WIDE), f32),
             pltpu.VMEM((mps, 8, 128), f32),
             dma((3,)),
             dma((heads, slots)),
+            dma((4, heads)),
+            dma((4, heads)),
+            dma((heads,)),
+            dma((heads,)),
             dma((2, heads)),
             dma((2, heads)),
-            dma((2,)),
-            dma((2,)),
-            dma((heads,)),
-            dma((heads,)),
             dma((plane,)),
             dma((plane,)),
             dma((mps,)),
@@ -588,7 +657,14 @@
         out_shape=results,
         in_specs=[hbm] * 4,
         out_specs=(hbm,) * 4,
-        scratch_shapes=[dma((slots + 3,))],
+        scratch_shapes=[
+            pltpu.VMEM(queries.shape, bf16),
+            pltpu.VMEM(d_out.shape, bf16),
+            pltpu.VMEM(neighbour_kv.shape[1:], bf16),
+            pltpu.VMEM(bias.shape, f32),
+            dma((slots + 3,)),
+            dma((slots + 3,)),
+        ],
         compiler_params=pltpu.CompilerParams(vmem_limit_bytes=VMEM_USE),
     )(*parts)
 

time: 71 us -> 33.1 us (0.47)
  Pallas kernels: 70.2 us -> 32.3 us
    pallas_call x1, Pallas kernels: 41 us -> 2.12 us  [pair_exchange(): pl.pallas_call(write_kernel, out_shape=results, in_specs=[hbm] * 4, out_s...]
    pallas_call x1, Pallas kernels: 29.2 us -> 30.2 us  [pair_exchange(): pl.pallas_call(pair_kernel, out_shape=results, in_specs=[hbm, hbm, hbm, h...]
where the time goes in v4:
time: 33.1 us; the launch traced here: 32.9 us
  Pallas kernels  32.3 us (98%)
  between operations  0.64 us (2%)
    pallas_call x1, Pallas kernels, pair_exchange(): pl.pallas_call(pair_kernel, out_shape=results, in_specs=[hbm, hbm, hbm, h...  30.2 us
    pallas_call x1, Pallas kernels, pair_exchange(): pl.pallas_call(write_kernel, out_shape=results, in_specs=[hbm] * 4, out_s...  2.12 us

profile of v4, /device:TPU:0, one launch (start us, length us, event | category | flops | bytes accessed | tf_op | source)
XLA Modules:
  0.0 32.9 jit_solution(9732046121945562565)
XLA Ops:
  0.6 30.2 %shard_map.84 = (bf16[1,128,512]{2,1,0:T(8,128)(2,1)}, bf16[1,128,512]{2,1,0:T(8,128)(2,1)}, bf16[1,4,128,2,512]{4,3,2,1,0:T(2,128)(2,1)}, f32[4,191]{1,0:T(4,128)}) custom-call(bf16[1,128,512]{2,1,0:T(8,128)(2,1)} %q_hbm.1, bf16[1,128,512]{2,1,0:T(8,128)(2,1)} %g_hbm.1, bf16[1,4,128,2,512]{4,3,2,1,0:T(2,128)(2,1)} %kv_hbm.1, s32[1,4]{1,0:T(1,128)} %target_hbm.1, ...), custom_call_target="tpu_custom_call" | custom-call | tf_op jit(solution)/shard_map/pallas_call | solution.py:606
  30.8 2.1 %shard_map.85 = (bf16[1,128,512]{2,1,0:T(8,128)(2,1)}, bf16[1,128,512]{2,1,0:T(8,128)(2,1)}, bf16[1,4,128,2,512]{4,3,2,1,0:T(2,128)(2,1)}, f32[4,191]{1,0:T(4,128)}) custom-call(bf16[1,128,512]{2,1,0:T(8,128)(2,1)} %get-tuple-element.8.att, bf16[1,128,512]{2,1,0:T(8,128)(2,1)} %get-tuple-element.9.dq, bf16[1,4,128,2,512]{4,3,2,1,0:T(2,128)(2,1)} %get-tuple-element.10.dkv, ...), custom_call_target="tpu_custom_call" | custom-call | tf_op jit(solution)/shard_map/pallas_call | solution.py:655

commit v5 on v4

--- a/solution.py
+++ b/solution.py
@@ -223,12 +223,30 @@
     return lax.broadcasted_iota(jnp.int32, shape, axis)
 
 
+def one_hot(flags):
+    return jnp.where(flags, 1.0, 0.0).astype(jnp.bfloat16)
+
+
+def halves(x):
+    high = x.astype(jnp.bfloat16)
+    return high, (x - high.astype(jnp.float32)).astype(jnp.bfloat16)
+
+
+def dot_chosen(x, picker):
+    high, rest = halves(x)
+    left = x - high.astype(jnp.float32)
+    low = (left - rest.astype(jnp.float32)).astype(jnp.bfloat16)
+    wide = jnp.concatenate([p.astype(jnp.float32) for p in (high, rest, low)], axis=0)
+    out = dot(wide.astype(jnp.bfloat16), picker)
+    return out[:8] + out[8:16] + out[16:]
+
+
 def pair_kernel(
     q_hbm, g_hbm, kv_hbm, target_hbm, bias_ref,
     att_hbm, dq_hbm, dkv_hbm, dbias_ref,
     target_ref, q_ref, g_ref, kv_pairs, kv_ref, q_peer, g_peer,
     windows, weights, cotangents, mixed, rows_own, rows_send, rows_recv,
-    gather_ref, scatter_ref, turned_ref, dkv_pairs, att_ref, dq_ref,
+    gather_ref, scatter_ref, turned_ref, pick_ref, unmix_ref, bias_rows, dkv_pairs, att_ref, dq_ref,
     stat_send, stat_recv, raw_all, norm_all,
     own_sems, kv_sems, in_send, in_recv, stat_send_sems, stat_recv_sems, row_send_sems, row_recv_sems,
     raw_send_sems, raw_recv_sems, norm_send_sems, norm_recv_sems, out_sems, dkv_sems,
@@ -339,6 +357,14 @@
             kv_copy(h, r).start()
 
     each(heads, start_kv)
+    place = iota((2 * WIDE, WIDE), 0) + 2 * iota((2 * WIDE, WIDE), 1)
+    unmix_ref[...] = one_hot(place == 2 * rel - 1)
+    place = iota((WIDE, 2 * WIDE), 1) + 2 * iota((WIDE, 2 * WIDE), 0)
+    bias_rows[...] = jnp.zeros((8, WIDE), jnp.float32)
+    bias_rows[:heads, :rel] = bias_ref[...]
+    turned = dot_chosen(bias_rows[...], one_hot(place == 2 * (rel - 1)))
+    for h in range(heads):
+        turned_ref[h] = jnp.broadcast_to(turned[h : h + 1], (8, 2 * WIDE))
     pl.semaphore_wait(barrier, plane - 1 + mps - 1)
 
     def start_rows(h):
@@ -368,24 +394,16 @@
     def token_of(axis, shape):
         place = iota(shape, axis)
         return jnp.where(place < tok, tok * seq + place, tok * (1 - seq) + place - tok)
-
-    def one_hot(flags):
-        return jnp.where(flags, 1.0, 0.0).astype(jnp.bfloat16)
 
     for r in range(slots):
         rows = pl.ds(r * STRETCH, STRETCH)
         first = (STRETCH - 1) + STRETCH * (entries[r] // 2)
         flat = (STRETCH, 2 * tok)
         gather_ref[rows, :] = one_hot(token_of(1, flat) == iota(flat, 0) + first)
+        column = iota((2 * 128, 128), 0) % 128
+        pick_ref[:, pl.ds(r * 128, 128)] = one_hot(column == entries[r])
     scatter_ref[...] = gather_ref[...].T
-    turn = jnp.where(
-        iota((rel, 2 * WIDE), 1) == 2 * (rel - 1) - 2 * iota((rel, 2 * WIDE), 0), 1.0, 0.0
-    ).astype(jnp.float32)
-    turned = jnp.dot(
-        bias_ref[...], turn, preferred_element_type=jnp.float32, precision=lax.Precision.HIGHEST
-    )
-    for h in range(heads):
-        turned_ref[h] = jnp.broadcast_to(turned[h : h + 1], (8, 2 * WIDE))
+    ones = jnp.ones((WIDE, 128), jnp.bfloat16)
     odd = iota((STRETCH, WIDE), 1) % 2 == 1
     lane = iota((STRETCH, 128), 1)
 
@@ -421,10 +439,11 @@
             grad_prob = prod[STRETCH:]
             peak = jnp.max(scores, axis=1, keepdims=True)
             expd = jnp.exp(scores - peak)
-            total = jnp.sum(expd, axis=1, keepdims=True)
-            expd = pltpu.roll(expd, 1, 1)
-            inner = jnp.sum(expd * grad_prob, axis=1, keepdims=True)
-            weights[h, r] = expd
+            rolled = pltpu.roll(expd, 1, 1)
+            high, low = halves(jnp.concatenate([expd, rolled * grad_prob], axis=0))
+            sums = dot(high, ones) + dot(low, ones)
+            total, inner = sums[:STRETCH], sums[STRETCH:]
+            weights[h, r] = rolled
             cotangents[h, r] = grad_prob
             base = entries[r]
             table = jnp.where(lane == base, peak, table)
@@ -456,13 +475,15 @@
         mine_f, other_f = jnp.exp(table - top), jnp.exp(other_peak - top)
         denominator = mine_f * total + other_f * partner(total)
         inner = (mine_f * inner + other_f * partner(inner)) / denominator
-        norm = mine_f / denominator
+        stats = jnp.concatenate([mine_f / denominator, inner], axis=0)
+        stats = jnp.where(iota((2 * STRETCH, 128), 1) < 8, stats, 0.0)
+        spread = dot(jnp.concatenate(halves(stats), axis=1), pick_ref[...])
         bias_sum = jnp.zeros((STRETCH, WIDE), jnp.float32)
         parts = []
         for r in range(slots):
-            at = lane == entries[r]
-            factor = jnp.sum(jnp.where(at, norm, 0.0), axis=1, keepdims=True)
-            shift = jnp.sum(jnp.where(at, inner, 0.0), axis=1, keepdims=True)
+            slot = spread[:, r * 128 : (r + 1) * 128]
+            slot = jnp.concatenate([slot, slot], axis=1)
+            factor, shift = slot[:STRETCH], slot[STRETCH:]
             prob = weights[h, r] * factor
             grad = prob * (cotangents[h, r] - shift)
             bias_sum = bias_sum + grad
@@ -497,12 +518,7 @@
     forward(0)
     stacked = lax.fori_loop(0, heads - 1, both, jnp.zeros((8, 2 * WIDE), jnp.float32))
     stacked = backward(heads - 1, stacked)
-    unmix = jnp.where(
-        iota((2 * WIDE, WIDE), 0) == 2 * rel - 1 - 2 * iota((2 * WIDE, WIDE), 1), 1.0, 0.0
-    ).astype(jnp.float32)
-    raw_all[here] = jnp.dot(
-        stacked, unmix, preferred_element_type=jnp.float32, precision=lax.Precision.HIGHEST
-    )
+    raw_all[here] = dot_chosen(stacked, unmix_ref[...])
     for k in range(1, plane):
         raw_copy(k).start()
 
@@ -626,6 +642,9 @@
             pltpu.VMEM((slots * STRETCH, 2 * tok), bf16),
             pltpu.VMEM((2 * tok, slots * STRETCH), bf16),
             pltpu.VMEM((heads, 8, 2 * WIDE), f32),
+            pltpu.VMEM((2 * 128, slots * 128), bf16),
+            pltpu.VMEM((2 * WIDE, WIDE), bf16),
+            pltpu.VMEM((8, WIDE), f32),
             pltpu.VMEM((heads, slots, NB_LEN, 2, depth), bf16),
             pltpu.VMEM((tok, width), bf16),
             pltpu.VMEM((tok, width), bf16),

time: 33.1 us -> 34.3 us (1.036)
  Pallas kernels: 32.3 us -> 33.5 us
    pallas_call x1, Pallas kernels: 30.2 us -> 31.4 us  [pair_exchange(): pl.pallas_call(pair_kernel, out_shape=results, in_specs=[hbm, hbm, hbm, h...]
where the time goes in v5:
time: 34.3 us; the launch traced here: 34.1 us
  Pallas kernels  33.5 us (98%)
  between operations  0.64 us (2%)
    pallas_call x1, Pallas kernels, pair_exchange(): pl.pallas_call(pair_kernel, out_shape=results, in_specs=[hbm, hbm, hbm, h...  31.4 us
    pallas_call x1, Pallas kernels, pair_exchange(): pl.pallas_call(write_kernel, out_shape=results, in_specs=[hbm] * 4, out_s...  2.12 us

profile of v5, /device:TPU:0, one launch (start us, length us, event | category | flops | bytes accessed | tf_op | source)
XLA Modules:
  0.0 34.1 jit_solution(5392331706945882386)
XLA Ops:
  0.6 31.4 %shard_map.84 = (bf16[1,128,512]{2,1,0:T(8,128)(2,1)}, bf16[1,128,512]{2,1,0:T(8,128)(2,1)}, bf16[1,4,128,2,512]{4,3,2,1,0:T(2,128)(2,1)}, f32[4,191]{1,0:T(4,128)}) custom-call(bf16[1,128,512]{2,1,0:T(8,128)(2,1)} %q_hbm.1, bf16[1,128,512]{2,1,0:T(8,128)(2,1)} %g_hbm.1, bf16[1,4,128,2,512]{4,3,2,1,0:T(2,128)(2,1)} %kv_hbm.1, s32[1,4]{1,0:T(1,128)} %target_hbm.1, ...), custom_call_target="tpu_custom_call" | custom-call | tf_op jit(solution)/shard_map/pallas_call | solution.py:622
  32.0 2.1 %shard_map.85 = (bf16[1,128,512]{2,1,0:T(8,128)(2,1)}, bf16[1,128,512]{2,1,0:T(8,128)(2,1)}, bf16[1,4,128,2,512]{4,3,2,1,0:T(2,128)(2,1)}, f32[4,191]{1,0:T(4,128)}) custom-call(bf16[1,128,512]{2,1,0:T(8,128)(2,1)} %get-tuple-element.8.att, bf16[1,128,512]{2,1,0:T(8,128)(2,1)} %get-tuple-element.9.dq, bf16[1,4,128,2,512]{4,3,2,1,0:T(2,128)(2,1)} %get-tuple-element.10.dkv, ...), custom_call_target="tpu_custom_call" | custom-call | tf_op jit(solution)/shard_map/pallas_call | solution.py:674

commit v6 on v5

--- a/solution.py
+++ b/solution.py
@@ -246,7 +246,7 @@
     att_hbm, dq_hbm, dkv_hbm, dbias_ref,
     target_ref, q_ref, g_ref, kv_pairs, kv_ref, q_peer, g_peer,
     windows, weights, cotangents, mixed, rows_own, rows_send, rows_recv,
-    gather_ref, scatter_ref, turned_ref, pick_ref, unmix_ref, bias_rows, dkv_pairs, att_ref, dq_ref,
+    gather_ref, scatter_ref, turned_ref, unmix_ref, bias_rows, dkv_pairs, att_ref, dq_ref,
     stat_send, stat_recv, raw_all, norm_all,
     own_sems, kv_sems, in_send, in_recv, stat_send_sems, stat_recv_sems, row_send_sems, row_recv_sems,
     raw_send_sems, raw_recv_sems, norm_send_sems, norm_recv_sems, out_sems, dkv_sems,
@@ -279,7 +279,7 @@
         )
 
     def cols(h):
-        return pl.ds(pl.multiple_of(h * depth, depth), depth)
+        return pl.ds(h * depth, depth)
 
     def q_copy(h, rows, lane):
         return remote(
@@ -333,11 +333,8 @@
         )
 
     def each(count, body):
-        def step(i, carry):
+        for i in range(count):
             body(i)
-            return carry
-
-        lax.fori_loop(0, count, step, 0)
 
     barrier = pltpu.get_barrier_semaphore()
     for step in range(1, plane):
@@ -400,10 +397,7 @@
         first = (STRETCH - 1) + STRETCH * (entries[r] // 2)
         flat = (STRETCH, 2 * tok)
         gather_ref[rows, :] = one_hot(token_of(1, flat) == iota(flat, 0) + first)
-        column = iota((2 * 128, 128), 0) % 128
-        pick_ref[:, pl.ds(r * 128, 128)] = one_hot(column == entries[r])
     scatter_ref[...] = gather_ref[...].T
-    ones = jnp.ones((WIDE, 128), jnp.bfloat16)
     odd = iota((STRETCH, WIDE), 1) % 2 == 1
     lane = iota((STRETCH, 128), 1)
 
@@ -439,11 +433,10 @@
             grad_prob = prod[STRETCH:]
             peak = jnp.max(scores, axis=1, keepdims=True)
             expd = jnp.exp(scores - peak)
-            rolled = pltpu.roll(expd, 1, 1)
-            high, low = halves(jnp.concatenate([expd, rolled * grad_prob], axis=0))
-            sums = dot(high, ones) + dot(low, ones)
-            total, inner = sums[:STRETCH], sums[STRETCH:]
-            weights[h, r] = rolled
+            total = jnp.sum(expd, axis=1, keepdims=True)
+            expd = pltpu.roll(expd, 1, 1)
+            inner = jnp.sum(expd * grad_prob, axis=1, keepdims=True)
+            weights[h, r] = expd
             cotangents[h, r] = grad_prob
             base = entries[r]
             table = jnp.where(lane == base, peak, table)
@@ -475,15 +468,13 @@
         mine_f, other_f = jnp.exp(table - top), jnp.exp(other_peak - top)
         denominator = mine_f * total + other_f * partner(total)
         inner = (mine_f * inner + other_f * partner(inner)) / denominator
-        stats = jnp.concatenate([mine_f / denominator, inner], axis=0)
-        stats = jnp.where(iota((2 * STRETCH, 128), 1) < 8, stats, 0.0)
-        spread = dot(jnp.concatenate(halves(stats), axis=1), pick_ref[...])
+        norm = mine_f / denominator
         bias_sum = jnp.zeros((STRETCH, WIDE), jnp.float32)
         parts = []
         for r in range(slots):
-            slot = spread[:, r * 128 : (r + 1) * 128]
-            slot = jnp.concatenate([slot, slot], axis=1)
-            factor, shift = slot[:STRETCH], slot[STRETCH:]
+            at = lane == entries[r]
+            factor = jnp.sum(jnp.where(at, norm, 0.0), axis=1, keepdims=True)
+            shift = jnp.sum(jnp.where(at, inner, 0.0), axis=1, keepdims=True)
             prob = weights[h, r] * factor
             grad = prob * (cotangents[h, r] - shift)
             bias_sum = bias_sum + grad
@@ -511,13 +502,12 @@
             folded = jnp.where((row8 // bit) % 2 == 0, pltpu.roll(folded, 2 * bit, 1), folded)
         return jnp.where(row8 == h, jnp.sum(folded, axis=0, keepdims=True), stacked)
 
-    def both(h, stacked):
-        forward(h + 1)
-        return backward(h, stacked)
-
+    stacked = jnp.zeros((8, 2 * WIDE), jnp.float32)
     forward(0)
-    stacked = lax.fori_loop(0, heads - 1, both, jnp.zeros((8, 2 * WIDE), jnp.float32))
-    stacked = backward(heads - 1, stacked)
+    for h in range(heads):
+        if h + 1 < heads:
+            forward(h + 1)
+        stacked = backward(h, stacked)
     raw_all[here] = dot_chosen(stacked, unmix_ref[...])
     for k in range(1, plane):
         raw_copy(k).start()
@@ -642,7 +632,6 @@
             pltpu.VMEM((slots * STRETCH, 2 * tok), bf16),
             pltpu.VMEM((2 * tok, slots * STRETCH), bf16),
             pltpu.VMEM((heads, 8, 2 * WIDE), f32),
-            pltpu.VMEM((2 * 128, slots * 128), bf16),
             pltpu.VMEM((2 * WIDE, WIDE), bf16),
             pltpu.VMEM((8, WIDE), f32),
             pltpu.VMEM((heads, slots, NB_LEN, 2, depth), bf16),

time: 34.3 us -> 32.8 us (0.956)
  Pallas kernels: 33.5 us -> 32 us
    pallas_call x1, Pallas kernels: 31.4 us -> 29.9 us  [pair_exchange(): pl.pallas_call(pair_kernel, out_shape=results, in_specs=[hbm, hbm, hbm, h...]
where the time goes in v6:
time: 32.8 us; the launch traced here: 32.7 us
  Pallas kernels  32 us (98%)
  between operations  0.64 us (2%)
    pallas_call x1, Pallas kernels, pair_exchange(): pl.pallas_call(pair_kernel, out_shape=results, in_specs=[hbm, hbm, hbm, h...  29.9 us
    pallas_call x1, Pallas kernels, pair_exchange(): pl.pallas_call(write_kernel, out_shape=results, in_specs=[hbm] * 4, out_s...  2.12 us

profile of v6, /device:TPU:0, one launch (start us, length us, event | category | flops | bytes accessed | tf_op | source)
XLA Modules:
  0.0 32.7 jit_solution(11241203734280108903)
XLA Ops:
  0.6 29.9 %shard_map.84 = (bf16[1,128,512]{2,1,0:T(8,128)(2,1)}, bf16[1,128,512]{2,1,0:T(8,128)(2,1)}, bf16[1,4,128,2,512]{4,3,2,1,0:T(2,128)(2,1)}, f32[4,191]{1,0:T(4,128)}) custom-call(bf16[1,128,512]{2,1,0:T(8,128)(2,1)} %q_hbm.1, bf16[1,128,512]{2,1,0:T(8,128)(2,1)} %g_hbm.1, bf16[1,4,128,2,512]{4,3,2,1,0:T(2,128)(2,1)} %kv_hbm.1, s32[1,4]{1,0:T(1,128)} %target_hbm.1, ...), custom_call_target="tpu_custom_call" | custom-call | tf_op jit(solution)/shard_map/pallas_call | solution.py:612
  30.5 2.1 %shard_map.85 = (bf16[1,128,512]{2,1,0:T(8,128)(2,1)}, bf16[1,128,512]{2,1,0:T(8,128)(2,1)}, bf16[1,4,128,2,512]{4,3,2,1,0:T(2,128)(2,1)}, f32[4,191]{1,0:T(4,128)}) custom-call(bf16[1,128,512]{2,1,0:T(8,128)(2,1)} %get-tuple-element.8.att, bf16[1,128,512]{2,1,0:T(8,128)(2,1)} %get-tuple-element.9.dq, bf16[1,4,128,2,512]{4,3,2,1,0:T(2,128)(2,1)} %get-tuple-element.10.dkv, ...), custom_call_target="tpu_custom_call" | custom-call | tf_op jit(solution)/shard_map/pallas_call | solution.py:663

commit v7 on v6

--- a/solution.py
+++ b/solution.py
@@ -246,7 +246,7 @@
     att_hbm, dq_hbm, dkv_hbm, dbias_ref,
     target_ref, q_ref, g_ref, kv_pairs, kv_ref, q_peer, g_peer,
     windows, weights, cotangents, mixed, rows_own, rows_send, rows_recv,
-    gather_ref, scatter_ref, turned_ref, unmix_ref, bias_rows, dkv_pairs, att_ref, dq_ref,
+    gather_ref, scatter_ref, turned_ref, kv_turned, grids, unmix_ref, bias_rows, dkv_pairs, att_ref, dq_ref,
     stat_send, stat_recv, raw_all, norm_all,
     own_sems, kv_sems, in_send, in_recv, stat_send_sems, stat_recv_sems, row_send_sems, row_recv_sems,
     raw_send_sems, raw_recv_sems, norm_send_sems, norm_recv_sems, out_sems, dkv_sems,
@@ -404,15 +404,17 @@
     def unpair(h):
         for r in range(slots):
             kv_copy(h, r).wait()
-            kv_ref[r, h] = kv_pairs[h, r].reshape(WIDE, depth)
+            block = kv_pairs[h, r].reshape(WIDE, depth)
+            kv_ref[r, h] = block
+            kv_turned[r, h] = block.T
+        wide = jnp.broadcast_to(turned_ref[h][:1], (STRETCH, 2 * WIDE))
+        grid = pltpu.roll(wide, 2 * WIDE - 126, 1, stride=2, stride_axis=0)[:, :WIDE]
+        grids[h] = jnp.where(odd, -1e30, grid)
 
     each(heads, unpair)
 
     def forward(h):
         table = jnp.zeros((STRETCH, 128), jnp.float32)
-        wide = jnp.broadcast_to(turned_ref[h][:1], (STRETCH, 2 * WIDE))
-        grid = pltpu.roll(wide, 2 * WIDE - 126, 1, stride=2, stride_axis=0)[:, :WIDE]
-        grid = jnp.where(odd, -1e30, grid)
         mine = jnp.concatenate([q_ref[:, cols(h)], g_ref[:, cols(h)]], axis=1)
         for copy in in_late(h):
             copy.wait_recv()
@@ -428,8 +430,8 @@
             rows = picked[r * STRETCH : (r + 1) * STRETCH]
             both = jnp.concatenate([rows[:, :depth], rows[:, depth:]], axis=0)
             windows[h, r] = both
-            prod = dot(both, kv_ref[r, h], ((1,), (1,)))
-            scores = prod[:STRETCH] * scale + grid
+            prod = dot(both, kv_turned[r, h])
+            scores = prod[:STRETCH] * scale + grids[h]
             grad_prob = prod[STRETCH:]
             peak = jnp.max(scores, axis=1, keepdims=True)
             expd = jnp.exp(scores - peak)
@@ -632,6 +634,8 @@
             pltpu.VMEM((slots * STRETCH, 2 * tok), bf16),
             pltpu.VMEM((2 * tok, slots * STRETCH), bf16),
             pltpu.VMEM((heads, 8, 2 * WIDE), f32),
+            pltpu.VMEM((slots, heads, depth, WIDE), bf16),
+            pltpu.VMEM((heads, STRETCH, WIDE), f32),
             pltpu.VMEM((2 * WIDE, WIDE), bf16),
             pltpu.VMEM((8, WIDE), f32),
             pltpu.VMEM((heads, slots, NB_LEN, 2, depth), bf16),

time: 32.8 us -> 32.7 us (level)
  no operation moved by 1% of the time
where the time goes in v7:
time: 32.7 us; the launch traced here: 32.5 us
  Pallas kernels  31.9 us (98%)
  between operations  0.64 us (2%)
    pallas_call x1, Pallas kernels, pair_exchange(): pl.pallas_call(pair_kernel, out_shape=results, in_specs=[hbm, hbm, hbm, h...  29.8 us
    pallas_call x1, Pallas kernels, pair_exchange(): pl.pallas_call(write_kernel, out_shape=results, in_specs=[hbm] * 4, out_s...  2.12 us

profile of v7, /device:TPU:0, one launch (start us, length us, event | category | flops | bytes accessed | tf_op | source)
XLA Modules:
  0.0 32.5 jit_solution(12132444872127685292)
XLA Ops:
  0.6 29.8 %shard_map.84 = (bf16[1,128,512]{2,1,0:T(8,128)(2,1)}, bf16[1,128,512]{2,1,0:T(8,128)(2,1)}, bf16[1,4,128,2,512]{4,3,2,1,0:T(2,128)(2,1)}, f32[4,191]{1,0:T(4,128)}) custom-call(bf16[1,128,512]{2,1,0:T(8,128)(2,1)} %q_hbm.1, bf16[1,128,512]{2,1,0:T(8,128)(2,1)} %g_hbm.1, bf16[1,4,128,2,512]{4,3,2,1,0:T(2,128)(2,1)} %kv_hbm.1, s32[1,4]{1,0:T(1,128)} %target_hbm.1, ...), custom_call_target="tpu_custom_call" | custom-call | tf_op jit(solution)/shard_map/pallas_call | solution.py:614
  30.4 2.1 %shard_map.85 = (bf16[1,128,512]{2,1,0:T(8,128)(2,1)}, bf16[1,128,512]{2,1,0:T(8,128)(2,1)}, bf16[1,4,128,2,512]{4,3,2,1,0:T(2,128)(2,1)}, f32[4,191]{1,0:T(4,128)}) custom-call(bf16[1,128,512]{2,1,0:T(8,128)(2,1)} %get-tuple-element.8.att, bf16[1,128,512]{2,1,0:T(8,128)(2,1)} %get-tuple-element.9.dq, bf16[1,4,128,2,512]{4,3,2,1,0:T(2,128)(2,1)} %get-tuple-element.10.dkv, ...), custom_call_target="tpu_custom_call" | custom-call | tf_op jit(solution)/shard_map/pallas_call | solution.py:667
